TPU v7x, 256 devices: a whole 4x4x8 slice. The times are simulated.
256 devices in a mesh: side: 2 (over core), head: 64 (over z, x_lo, y), sub: 2 (over x_hi).
Axes of the slice: x: 4 (x_hi: 2, x_lo: 2; x = x_hi * 2 + x_lo), y: 4, z: 8, core: 2. Of those that a mesh axis runs over, the one named last changes fastest.
Arguments:
- queries: bfloat16 [2, 512, 64, 576], P('sub', None, 'head'), may hold values from -1500 to 1500
- cache_pool: bfloat16 [2, 1024, 64, 576], P('sub', 'head'), may hold values from -7 to 7
- block_table: int32 [2, 512, 2], P('sub', 'head'), may hold values from 0 to 15, as said below
- cache_len: int32 [2, 512], P('sub', 'head'), may hold values from 1 to 128, 32768 in all within a row
- w_uv: bfloat16 [64, 512, 128], P('head'), may hold values from -0.75 to 0.75
- w_out: bfloat16 [64, 128, 7168], P('head'), may hold values from -0.125 to 0.125
- residual: bfloat16 [2, 512, 7168], P('sub', 'head'), may hold values from -6 to 6
- norm_gain: float32 [7168], replicated, may hold values from 0.1 to 1.9
- expert_ids: int32 [2, 512, 4], P('sub', 'head'), may hold values from 0 to 7, all different within a row; in each aligned block of 8 rows (0 to 7, 8 to 15, ..., all dimensions but the last counted through in order) at most 8 rows name the same one
- expert_gates: float32 [2, 512, 4], P('sub', 'head'), may hold values from 0.1 to 1
- w_gate: bfloat16 [64, 7168, 128], P('head'), may hold values from -0.0625 to 0.0625
- w_up: bfloat16 [64, 7168, 128], P('head'), may hold values from -0.0625 to 0.0625
- w_down: bfloat16 [64, 128, 7168], P('head'), may hold values from -0.375 to 0.375
Outputs:
- layer_out: bfloat16 [2, 2, 512, 7168], P('side', 'sub', 'head')
Inputs may be any that keep to these rules, and one draw needn't show every extreme that they name: `block_table`: the block table entries of the 8 rows of one owner name each of that owner's 16 blocks exactly once. `cache_len`: the 512 lengths of each half sum to 32768, and the longest is 128. `expert_ids`: each row names 4 different experts; the 8 rows of one device name one expert at most 8 times, and that bound is reached.
All inputs are finite; a program needn't handle non-finite values. No bound on the sum of `cache_len` on one device may be relied on, other than what follows from the above.
Results may differ from a plain program's by a relative error of at most 0.009.
Values may be sent and summed in bfloat16 or wider, within the bound.
A program may use at most 192 MiB of HBM per device.

v0:
```python
import jax
import jax.numpy as jnp
from jax import lax
from jax.sharding import PartitionSpec as P

LAT = 512
FFW = 1024


score_scale = 192 ** (-0.5)


def passed_along(block, axis, distance):
    devices = range(lax.axis_size(axis))
    route = [(i - distance, i) for i in devices if i - distance in devices]
    return lax.ppermute(block, axis, route)


def attend(query, key_rows, visible):
    scores = (
        jnp.einsum("nhk,nlk->nhl", query, key_rows, preferred_element_type=jnp.float32)
        * score_scale
    )
    shown = visible[:, None, :]
    scores = jnp.where(shown, scores, -1e30)
    peak = jnp.max(scores, axis=-1)
    raw_weights = jnp.exp(scores - peak[..., None]) * shown.astype(jnp.float32)
    weight_sum = jnp.sum(raw_weights, axis=-1)
    accumulated = jnp.einsum(
        "nhl,nlc->nhc",
        raw_weights,
        key_rows[:, :, :LAT].astype(jnp.float32),
        precision=lax.Precision.HIGHEST,
    )
    return (peak, weight_sum, accumulated)


def slot_layout(expert_ids, expert_count, capacity):
    picked = expert_ids[:, :, None] == jnp.arange(expert_count, dtype=jnp.int32)[None, None, :]
    member = jnp.any(picked, axis=1)
    member_int = member.astype(jnp.int32)
    slot_rank = jnp.cumsum(member_int, axis=0) - member_int
    onehot = member[:, :, None] & (
        slot_rank[:, :, None] == jnp.arange(capacity, dtype=jnp.int32)[None, None, :]
    )
    return (picked, onehot)


def pack_rows(rows_in, onehot, piece_count):
    chosen = onehot.astype(jnp.bfloat16)
    buffer = jnp.einsum("jec,jd->ecd", chosen, rows_in, preferred_element_type=jnp.float32).astype(
        jnp.bfloat16
    )
    return jnp.repeat(buffer, piece_count, axis=0)


def per_device(
    queries,
    cache_pool,
    block_table,
    cache_len,
    w_uv,
    w_out,
    residual,
    norm_gain,
    expert_ids,
    expert_gates,
    w_gate,
    w_up,
    w_down,
):
    side_index = lax.axis_index("side")
    attend_flag = side_index == 0
    expert_flag = side_index == 1
    head_count = lax.axis_size("head")
    piece_count = FFW // w_gate.shape[2]
    query = queries[0, :, 0, :]
    half_rows = query.shape[0]
    own_rows = half_rows // head_count
    owner_table = block_table[0]
    lengths = cache_len[0]
    pool_part = cache_pool[0]
    block_len = pool_part.shape[1]
    row_blocks = owner_table.shape[1]
    positions = jnp.arange(row_blocks * block_len, dtype=jnp.int32)
    owner_queries = lax.all_to_all(queries[0], "head", split_axis=0, concat_axis=1, tiled=True)
    key_rows = pool_part[owner_table].reshape(own_rows, row_blocks * block_len, -1)
    visible = positions[None, :] < lengths[:, None]

    def local_attention(operand):
        peak, weight_sum, accumulated = attend(operand, key_rows, visible)
        return (accumulated / weight_sum[..., None]).astype(jnp.bfloat16)

    def no_attention(operand):
        return jnp.zeros((operand.shape[0], operand.shape[1], LAT), jnp.bfloat16)

    own_latents = lax.cond(attend_flag, local_attention, no_attention, owner_queries)
    latents = lax.all_to_all(own_latents, "head", split_axis=1, concat_axis=0, tiled=True)[:, 0, :]
    head_out = jnp.dot(latents, w_uv[0], preferred_element_type=jnp.float32).astype(jnp.bfloat16)
    attended = lax.psum_scatter(
        jnp.dot(head_out, w_out[0], preferred_element_type=jnp.float32),
        "head",
        scatter_dimension=0,
        tiled=True,
    )
    stream = (residual[0].astype(jnp.float32) + attended).astype(jnp.bfloat16)
    stream_f = stream.astype(jnp.float32)
    mean_square = jnp.mean(stream_f * stream_f, axis=-1, keepdims=True)
    normed = (stream_f * lax.rsqrt(mean_square + 1e-06) * norm_gain).astype(jnp.bfloat16)
    row_ids = expert_ids[0]
    row_gates = expert_gates[0]
    expert_count = head_count // piece_count
    top_count = row_ids.shape[1]
    capacity = min(own_rows, max(2, 2 * own_rows * top_count // expert_count))
    picked, onehot = slot_layout(row_ids, expert_count, capacity)

    def expert_ffn(received):
        gate_part = jnp.einsum(
            "sid,du->siu", received, w_gate[0], preferred_element_type=jnp.float32
        )
        up_part = jnp.einsum("sid,du->siu", received, w_up[0], preferred_element_type=jnp.float32)
        hidden = (jax.nn.silu(gate_part) * up_part).astype(jnp.bfloat16)
        return jnp.einsum(
            "siu,ud->sid", hidden, w_down[0], preferred_element_type=jnp.float32
        ).astype(jnp.bfloat16)

    far_rows = passed_along(normed, "side", 1)
    outgoing = pack_rows(far_rows, onehot, piece_count)
    returned = lax.all_to_all(
        lax.cond(
            expert_flag,
            expert_ffn,
            lambda operand: jnp.zeros_like(operand),
            lax.all_to_all(outgoing, "head", split_axis=0, concat_axis=0, tiled=True),
        ),
        "head",
        split_axis=0,
        concat_axis=0,
        tiled=True,
    )
    summed = jnp.sum(
        returned.reshape(expert_count, piece_count, capacity, -1).astype(jnp.float32), axis=1
    )
    selection = jnp.sum(row_gates[:, :, None] * picked.astype(jnp.float32), axis=1)
    mixing = (selection[:, :, None] * onehot.astype(jnp.float32)).reshape(
        own_rows, expert_count * capacity
    )
    mixture = jnp.dot(
        mixing, summed.reshape(expert_count * capacity, -1), precision=lax.Precision.HIGHEST
    )
    result = jnp.where(attend_flag, stream, mixture.astype(jnp.bfloat16))
    return result[None, None]


def solution(mesh):
    in_specs = (
        P("sub", None, "head", None),
        P("sub", "head", None, None),
        P("sub", "head", None),
        P("sub", "head"),
        P("head", None, None),
        P("head", None, None),
        P("sub", "head", None),
        P(),
        P("sub", "head", None),
        P("sub", "head", None),
        P("head", None, None),
        P("head", None, None),
        P("head", None, None),
    )
    out_specs = P("side", "sub", "head", None)
    return jax.shard_map(
        per_device, mesh=mesh, in_specs=in_specs, out_specs=out_specs, check_vma=False
    )
```

profile of v0, /device:TPU:25, one launch (start us, length us, event | category | flops | bytes accessed | tf_op | source)
XLA Modules:
  0.0 795.5 jit_solution(2146997872830680750)
XLA Ops:
  6.5 0.5 broadcast.88
  7.0 2.2 reduce
  9.5 1.5 reshape.87
  11.0 12.4 %all-to-all-start = ((bf16[64,2,2304]{2,1,0:T(2,128)(2,1)}), bf16[64,2,2304]{2,1,0:T(2,128)(2,1)}, u32[]{:S(2)}, u32[]{:S(2)}) async-start(bf16[64,2,2304]{2,1,0:T(2,128)(2,1)} %reshape.87), calls=%async_computation | async-start | bytes 1179648 | tf_op jit(solution)/shard_map/all_to_all | solution.py:86
  23.5 16.2 %all-to-all-done = bf16[64,2,2304]{2,1,0:T(2,128)(2,1)} async-done(((bf16[64,2,2304]{2,1,0:T(2,128)(2,1)}), bf16[64,2,2304]{2,1,0:T(2,128)(2,1)}, u32[]{:S(2)}, u32[]{:S(2)}) %all-to-all-start) | async-done | bytes 589856 | tf_op jit(solution)/shard_map/all_to_all | solution.py:86
  39.7 4.3 reshape.88
  43.9 1.0 copy.68
  45.3 19.9 %all_to_all.45 = bf16[8,64,512]{2,0,1:T(8,128)(2,1)S(1)} all-to-all(bf16[8,64,512]{2,0,1:T(8,128)(2,1)S(1)} %copy.53), channel_id=1, replica_groups=mesh['side'=2,'head'=64,'sub'=2] {'head'}, dimensions={1} | all-to-all | bytes 1048576 | tf_op jit(solution)/shard_map/all_to_all | solution.py:98
  65.2 6.5 fusion.32
  71.7 0.7 copy-done.5
  72.5 298.7 %reduce-scatter.2.cloned.1.call-done = f32[8,7168]{1,0:T(8,128)} async-done(((f32[512,7168]{1,0:T(8,128)}), f32[8,7168]{1,0:T(8,128)}) %reduce-scatter.2.cloned.1.call-update) | async-done | bytes 229392 | tf_op jit(solution)/shard_map/reduce_scatter | solution.py:100
  371.3 1.1 fusion.36
  372.5 1.3 collective-permute-start
  373.9 47.2 %collective-permute-done = bf16[8,7168]{1,0:T(8,128)(2,1)S(1)} collective-permute-done((bf16[8,7168]{1,0:T(8,128)(2,1)S(1)}, bf16[8,7168]{1,0:T(8,128)(2,1)S(1)}, u32[]{:S(2)}, u32[]{:S(2)}) %collective-permute-start) | collective-permute-done | bytes 114720 | tf_op jit(solution)/shard_map/ppermute | solution.py:16
  421.6 3.9 broadcast_in_dim.23
  425.5 15.3 %all-to-all-start.2 = ((bf16[64,8,7168]{2,1,0:T(8,128)(2,1)}), bf16[64,8,7168]{2,1,0:T(8,128)(2,1)}, u32[]{:S(2)}, u32[]{:S(2)}) async-start(bf16[64,8,7168]{2,1,0:T(8,128)(2,1)} %bitcast.80), calls=%async_computation.3 | async-start | bytes 14680064 | tf_op jit(solution)/shard_map/all_to_all | solution.py:134
  440.8 160.8 %all-to-all-done.2 = bf16[64,8,7168]{2,1,0:T(8,128)(2,1)} async-done(((bf16[64,8,7168]{2,1,0:T(8,128)(2,1)}), bf16[64,8,7168]{2,1,0:T(8,128)(2,1)}, u32[]{:S(2)}, u32[]{:S(2)}) %all-to-all-start.2) | async-done | bytes 7340064 | tf_op jit(solution)/shard_map/all_to_all | solution.py:134
  601.6 20.5 %conditional.3 = (bf16[64,8,7168]{2,1,0:T(8,128)(2,1)}) conditional(s32[]{:T(128)} %convert_element_type.74, () %tuple.26, (bf16[1,7168,128]{2,1,0:T(8,128)(2,1)}, bf16[64,8,7168]{2,1,0:T(8,128)(2,1)}, bf16[1,7168,128]{2,1,0:T(8,128)(2,1)}, bf16[1,128,7168]{2,1,0:T(8,128)(2,1)}) %tuple.27), branch_computations={%region_9.10_spmd, %region_10.11_spmd} | conditional | flops 2822635520 | bytes 28049416 | solution.py:130
  601.6 5.6 fusion.3
  607.2 14.9 %convolution_convert_fusion = bf16[64,8,7168]{2,1,0:T(8,128)(2,1)} fusion(bf16[1,128,7168]{2,1,0:T(8,128)(2,1)} %get-tuple-element.94, bf16[64,8,7168]{2,1,0:T(8,128)(2,1)} %get-tuple-element.79, bf16[1,7168,128]{2,1,0:T(8,128)(2,1)} %get-tuple-element.93, f32[64,8,128]{2,1,0:T(8,128)S(1)} %fusion.3), kind=kOutput, calls=%fused_computation.1 | convolution fusion | flops 1883111424 | bytes 18612224 | tf_op jit(solution)/shard_map/cond/branch_1_fun/siu,ud->sid/dot_general | solution.py:123
  622.1 10.2 %all-to-all-start.3 = ((bf16[64,8,7168]{2,1,0:T(8,128)(2,1)}), bf16[64,8,7168]{2,1,0:T(8,128)(2,1)}, u32[]{:S(2)}, u32[]{:S(2)}) async-start(bf16[64,8,7168]{2,1,0:T(8,128)(2,1)} %get-tuple-element.122), calls=%async_computation.4 | async-start | bytes 14680064 | tf_op jit(solution)/shard_map/all_to_all | solution.py:129
  632.5 147.6 %all-to-all-done.3 = bf16[64,8,7168]{2,1,0:T(8,128)(2,1)} async-done(((bf16[64,8,7168]{2,1,0:T(8,128)(2,1)}), bf16[64,8,7168]{2,1,0:T(8,128)(2,1)}, u32[]{:S(2)}, u32[]{:S(2)}) %all-to-all-start.3) | async-done | bytes 7340064 | tf_op jit(solution)/shard_map/all_to_all | solution.py:129
  780.0 4.5 convert_reduce_fusion
  784.5 4.1 fusion.31
  (33 shorter events, 1.8 us)
Async XLA Ops:
  6.5 58.7 %copy-start = (bf16[1,128,7168]{2,1,0:T(8,128)(2,1)S(1)}, bf16[1,128,7168]{2,1,0:T(8,128)(2,1)}, u32[]{:S(2)}) copy-start(bf16[1,128,7168]{2,1,0:T(8,128)(2,1)} %param.22) | copy-start | bytes 5505028
  11.0 28.6 %all-to-all-start = ((bf16[64,2,2304]{2,1,0:T(2,128)(2,1)}), bf16[64,2,2304]{2,1,0:T(2,128)(2,1)}, u32[]{:S(2)}, u32[]{:S(2)}) async-start(bf16[64,2,2304]{2,1,0:T(2,128)(2,1)} %reshape.87), calls=%async_computation | async-start | bytes 1179648 | tf_op jit(solution)/shard_map/all_to_all | solution.py:86
  23.4 347.8 %reduce-scatter.2.cloned.1.call-start = ((), (), s32[]{:S(2)}) async-start(), calls=%async_computation.5 | async-start | bytes 14909440 | tf_op jit(solution)/shard_map/reduce_scatter | solution.py:100
  23.5 21.4 %copy-start.7 = (s32[1,8,2]{1,2,0:T(2,128)S(1)}, s32[1,8,2]{1,2,0:T(2,128)}, u32[]{:S(2)}) copy-start(s32[1,8,2]{1,2,0:T(2,128)} %param.19) | copy-start | bytes 196
  23.5 21.4 %copy-start.8 = (s32[1,8]{1,0:T(1,128)S(1)}, s32[1,8]{1,0:T(1,128)}, u32[]{:S(2)}) copy-start(s32[1,8]{1,0:T(1,128)} %param.20) | copy-start | bytes 100
  45.0 20.2 %copy-start.2 = (bf16[1,512,128]{2,1,0:T(8,128)(2,1)S(1)}, bf16[1,512,128]{2,1,0:T(8,128)(2,1)}, u32[]{:S(2)}) copy-start(bf16[1,512,128]{2,1,0:T(8,128)(2,1)} %param.21) | copy-start | bytes 393220
  71.7 0.7 copy-start.5
  71.7 299.6 %copy-start.3 = (bf16[1,8,7168]{2,1,0:T(8,128)(2,1)S(1)}, bf16[1,8,7168]{2,1,0:T(8,128)(2,1)}, u32[]{:S(2)}) copy-start(bf16[1,8,7168]{2,1,0:T(8,128)(2,1)} %param.23) | copy-start | bytes 344068
  71.7 300.7 %copy-start.4 = (f32[7168]{0:T(1024)S(1)}, f32[7168]{0:T(1024)}, u32[]{:S(2)}) copy-start(f32[7168]{0:T(1024)} %param.24) | copy-start | bytes 86020
  372.5 48.6 %collective-permute-start = (bf16[8,7168]{1,0:T(8,128)(2,1)S(1)}, bf16[8,7168]{1,0:T(8,128)(2,1)S(1)}, u32[]{:S(2)}, u32[]{:S(2)}) collective-permute-start(bf16[8,7168]{1,0:T(8,128)(2,1)S(1)} %fusion.38), channel_id=1, source_target_pairs={{0,128},{1,129},{2,130},{3,131},{4,132},{5,133},{6,134},{7,135},{8... | collective-permute-start | bytes 344072 | tf_op jit(solution)/shard_map/ppermute | solution.py:16
  425.5 176.1 %all-to-all-start.2 = ((bf16[64,8,7168]{2,1,0:T(8,128)(2,1)}), bf16[64,8,7168]{2,1,0:T(8,128)(2,1)}, u32[]{:S(2)}, u32[]{:S(2)}) async-start(bf16[64,8,7168]{2,1,0:T(8,128)(2,1)} %bitcast.80), calls=%async_computation.3 | async-start | bytes 14680064 | tf_op jit(solution)/shard_map/all_to_all | solution.py:134
  622.1 10.2 %copy-start.6 = (f32[1,8,4]{1,2,0:T(4,128)S(1)}, f32[1,8,4]{1,2,0:T(4,128)}, u32[]{:S(2)}) copy-start(f32[1,8,4]{1,2,0:T(4,128)} %param.26) | copy-start | bytes 388
  622.1 158.0 %all-to-all-start.3 = ((bf16[64,8,7168]{2,1,0:T(8,128)(2,1)}), bf16[64,8,7168]{2,1,0:T(8,128)(2,1)}, u32[]{:S(2)}, u32[]{:S(2)}) async-start(bf16[64,8,7168]{2,1,0:T(8,128)(2,1)} %get-tuple-element.122), calls=%async_computation.4 | async-start | bytes 14680064 | tf_op jit(solution)/shard_map/all_to_all | solution.py:129
Sparse Core Ops, SparseCore 0:
  71.8 299.4 reduce-scatter.1
where the time goes:
time: 799 us; the launch traced here: 795 us
  waiting for transfers between devices  670 us (84%)
  starting transfers between devices  39.2 us (5%)
  matrix products  31.6 us (4%)
  blocking collectives  19.9 us (2%)
  between operations  13.6 us (2%)
  local copies, waits for them, and re-layouts  12.7 us (2%)
  other arithmetic  8.07 us (1%)
    reduce_scatter x1, waiting for transfers between devices, per_device(): lax.psum_scatter(jnp.dot(head_out, w_out[0], preferred_element_type=jnp.f...  299 us
    all_to_all x1, waiting for transfers between devices, per_device(): lax.all_to_all(outgoing, 'head', split_axis=0, concat_axis=0, tiled=True)  161 us
    all_to_all x1, waiting for transfers between devices, per_device(): lax.all_to_all(lax.cond(expert_flag, expert_ffn, lambda operand: jnp.zero...  148 us
    ppermute x1, waiting for transfers between devices, passed_along(): return lax.ppermute(block, axis, route)  47.2 us
    all_to_all x1, blocking collectives, per_device(): lax.all_to_all(own_latents, 'head', split_axis=1, concat_axis=0, tiled=True)  19.9 us
    all_to_all x1, waiting for transfers between devices, per_device(): lax.all_to_all(queries[0], 'head', split_axis=0, concat_axis=1, tiled=True)  16.2 us
  transfers between devices with their start and end apart: 5, of which 5 were waited for; matrix products, arithmetic and copies ran while one was open for 0% of the time, Pallas kernels for 0%

commit v1 on v0

v1 whole, which is shorter than its diff:
```python
import jax
import jax.numpy as jnp
from jax import lax
from jax.experimental import pallas as pl
from jax.experimental.pallas import tpu as pltpu
from jax.sharding import PartitionSpec as P

D = 7168
LAT = 512
KW = 576
VH = 128
UNITS = 128
EPS = 1e-6
SCALE = 192 ** (-0.5)

NZ = 8
NP = 8
NY = 4
OWN = 8
COLS = D // NP
CHUNK = NY * OWN
ROWS = NZ * CHUNK
NH = NZ * NY
F32 = jnp.float32
BF16 = jnp.bfloat16


def kernel(
    q_ref, pool_ref, tab_ref, len_ref, wuv_ref, wout_ref, res_ref, gain_ref,
    ids_ref, gates_ref, wg_ref, wu_ref, wd_ref,
    out_ref,
    pool, wuv, gain, qbuf, lat_out, lat_in, sel, resbuf, selbuf,
    wo, wgu, wd, head_own, head_all, c_out, c_in,
    stream_out, stream_in, ssq_own, ssq_in, rs_all, x_all,
    h_out, h_in, hid_own, hid_all, o_out, o_in, mix_out, mix_in,
    load, send, recv,
):
    c = lax.axis_index("side")
    h = lax.axis_index("head")
    sub = lax.axis_index("sub")
    z, n = h // NP, h % NP
    xl, y = n // NY, n % NY
    spot = z * NY + y

    def device(core, head):
        return (core, head, sub)

    def put(src, dst, phase, core, head):
        pltpu.make_async_remote_copy(
            src_ref=src, dst_ref=dst, send_sem=send.at[phase], recv_sem=recv.at[phase],
            device_id=device(core, head), device_id_type=pl.DeviceIdType.MESH,
        ).start()

    def keep(src, dst, phase):
        pltpu.make_async_copy(src, dst, recv.at[phase]).start()

    def arrived(ref, phase):
        pltpu.make_async_copy(ref, ref, recv.at[phase]).wait()

    def gone(ref, phase):
        pltpu.make_async_copy(ref, ref, send.at[phase]).wait()

    def loop(count, body):
        def step(k, carry):
            body(k)
            return carry
        lax.fori_loop(0, count, step, 0)

    def plane(k):
        return (n + k) % NP

    def depth(k):
        return (z + k) % NZ

    def cols(m):
        return pl.ds(pl.multiple_of(m * COLS, 128), COLS)

    Q, RES, SEL, LATS, WO, WOF, HEAD, C, STREAM, SSQ, RS, X, WG, WU, WGUF, WD, WDF, H, HID, O, MIX = range(21)

    def send_query(k):
        m = (k + spot) % NH
        owner = (m // NY) * NP + c * NY + m % NY
        put(q_ref.at[owner], qbuf.at[spot], Q, 1 - xl, owner)
    loop(NH, send_query)

    pltpu.make_async_copy(pool_ref, pool, load.at[0]).start()
    pltpu.make_async_copy(wuv_ref, wuv, load.at[1]).start()
    pltpu.make_async_copy(gain_ref.at[:, cols(n)], gain, load.at[2]).start()

    lane = lax.broadcasted_iota(jnp.int32, (OWN, 128), 1)
    picked = jnp.zeros((OWN, 128), F32)
    for k in range(ids_ref.shape[1]):
        picked = picked + jnp.where(ids_ref[:, k:k + 1] == lane, gates_ref[:, k:k + 1], 0.0)
    sel[...] = picked

    def send_residual(k):
        m = (1 - c) * NY + (y + k) % NY
        put(res_ref.at[:, cols(m)], resbuf.at[y], RES, xl, z * NP + m)
        put(sel, selbuf.at[y], SEL, xl, z * NP + m)
    loop(NY, send_residual)

    half_o = pl.ds(pl.multiple_of(c * (VH // 2), VH // 2), VH // 2)
    half_d = pl.ds(pl.multiple_of(c * (UNITS // 2), UNITS // 2), UNITS // 2)
    half_g = pl.ds(pl.multiple_of(c * (COLS // 2), COLS // 2), COLS // 2)

    keep(wout_ref.at[half_o, cols(n)], wo.at[n, half_o], WO)
    def send_wo(k):
        m = plane(k + 1)
        put(wout_ref.at[half_o, cols(m)], wo.at[n, half_o], WO, c, z * NP + m)
    loop(NP - 1, send_wo)

    def depth_rows(m):
        return pl.ds(pl.multiple_of(m * COLS + c * (COLS // 2), COLS // 2), COLS // 2)

    block = lax.broadcasted_iota(jnp.int32, (OWN, 1024), 1) // 64
    offset = lax.broadcasted_iota(jnp.int32, (OWN, 1024), 1) % 64
    row = lax.broadcasted_iota(jnp.int32, (OWN, 1024), 0)
    length = jnp.zeros((OWN, 1024), jnp.int32)
    for r in range(OWN):
        length = jnp.where(row == r, len_ref[r], length)
    seen = ((block == tab_ref[:, 0:1]) & (offset < length)) | (
        (block == tab_ref[:, 1:2]) & (offset + 64 < length))
    bias = jnp.where(seen, 0.0, -1e30).astype(F32)

    pltpu.make_async_copy(pool_ref, pool, load.at[0]).wait()
    arrived(qbuf, Q)
    queries = qbuf[...].astype(F32).reshape(NH * OWN, KW).astype(BF16)
    keys = pool[...].reshape(1024, KW)
    scores = lax.dot_general(
        queries, keys, (((1,), (1,)), ((), ())), preferred_element_type=F32)
    scores = scores.reshape(NH, OWN, 1024) * SCALE + bias[None]
    scores = scores.reshape(NH * OWN, 1024)
    peak = jnp.max(scores, axis=-1, keepdims=True)
    raw = jnp.exp(scores - peak)
    total = jnp.sum(raw, axis=-1, keepdims=True)
    latents = jnp.dot(raw.astype(BF16), keys[:, :LAT], preferred_element_type=F32) / total
    lat_out[...] = latents.reshape(NH, OWN, LAT).astype(BF16)

    def send_latent(k):
        m = (k + spot) % NH
        put(lat_out.at[m], lat_in.at[spot], LATS, xl, (m // NY) * NP + (1 - c) * NY + m % NY)
    loop(NH, send_latent)

    keep(wg_ref.at[depth_rows(n)], wgu.at[n, half_g, pl.ds(0, 128)], WG)
    keep(wu_ref.at[depth_rows(n)], wgu.at[n, half_g, pl.ds(128, 128)], WU)
    def send_wgu(k):
        m = plane(k + 1)
        put(wg_ref.at[depth_rows(m)], wgu.at[n, half_g, pl.ds(0, 128)], WG, c, z * NP + m)
        put(wu_ref.at[depth_rows(m)], wgu.at[n, half_g, pl.ds(128, 128)], WU, c, z * NP + m)
    loop(NP - 1, send_wgu)

    arrived(wo.at[:, half_o], WO)
    put(wo.at[:, half_o], wo.at[:, half_o], WOF, 1 - c, h)

    pltpu.make_async_copy(wuv_ref, wuv, load.at[1]).wait()
    arrived(lat_in, LATS)
    latent_rows = lat_in[...].astype(F32).reshape(ROWS, LAT).astype(BF16)
    head_own[...] = jnp.dot(latent_rows, wuv[...], preferred_element_type=F32).astype(BF16)
    keep(head_own, head_all.at[n], HEAD)
    def send_head(k):
        put(head_own, head_all.at[n], HEAD, c, z * NP + plane(k + 1))
    loop(NP - 1, send_head)

    arrived(wo.at[:, half_o], WOF)
    arrived(head_all, HEAD)
    heads = jnp.concatenate([head_all[i] for i in range(NP)], axis=1)
    partial = jnp.dot(heads, wo[...].reshape(NP * VH, COLS), preferred_element_type=F32)
    c_out[...] = partial.astype(BF16).reshape(NZ, CHUNK, COLS)
    keep(c_out.at[z], c_in.at[z], C)
    def send_c(k):
        m = depth(k + 1)
        put(c_out.at[m], c_in.at[z], C, c, m * NP + n)
    loop(NZ - 1, send_c)

    arrived(resbuf, RES)
    arrived(selbuf, SEL)
    pltpu.make_async_copy(gain_ref.at[:, cols(n)], gain, load.at[2]).wait()
    arrived(c_in, C)
    attended = c_in[0].astype(F32)
    for i in range(1, NZ):
        attended = attended + c_in[i].astype(F32)
    stream = (resbuf[...].astype(F32).reshape(CHUNK, COLS) + attended).astype(BF16).astype(F32)
    x_all[z] = (stream * gain[...]).astype(BF16)
    def send_x(k):
        put(x_all.at[z], x_all.at[z], X, c, depth(k + 1) * NP + n)
    loop(NZ - 1, send_x)

    ssq_own[...] = jnp.broadcast_to(jnp.sum(stream * stream, axis=-1, keepdims=True), (CHUNK, 128))
    keep(ssq_own, ssq_in.at[n], SSQ)
    def send_ssq(k):
        put(ssq_own, ssq_in.at[n], SSQ, c, z * NP + plane(k + 1))
    loop(NP - 1, send_ssq)

    stream_out[...] = stream.reshape(NY, OWN, COLS).astype(BF16)

    def home(core, src, landing, phase):
        def step(k):
            own = (c == core) & (xl == c) & (y == k)
            @pl.when(own)
            def _():
                keep(src.at[k], landing.at[n], phase)
            @pl.when(jnp.logical_not(own))
            def _():
                put(src.at[k], landing.at[n], phase, core, z * NP + c * NY + k)
        loop(NY, step)

    home(0, stream_out, stream_in, STREAM)

    arrived(ssq_in, SSQ)
    square = ssq_in[0]
    for i in range(1, NP):
        square = square + ssq_in[i]
    scale = lax.rsqrt(square * (1.0 / D) + EPS)
    wide = lax.broadcasted_iota(jnp.int32, (CHUNK, 128), 1)
    rs_all[z] = jnp.where(wide < 8, selbuf[...].reshape(CHUNK, 128), scale)
    def send_rs(k):
        put(rs_all.at[z], rs_all.at[z], RS, c, depth(k + 1) * NP + n)
    loop(NZ - 1, send_rs)

    arrived(wgu.at[:, half_g, pl.ds(0, 128)], WG)
    arrived(wgu.at[:, half_g, pl.ds(128, 128)], WU)
    put(wgu.at[:, half_g], wgu.at[:, half_g], WGUF, 1 - c, h)

    keep(wd_ref.at[half_d, cols(n)], wd.at[n, half_d], WD)
    def send_wd(k):
        m = plane(k + 1)
        put(wd_ref.at[half_d, cols(m)], wd.at[n, half_d], WD, c, z * NP + m)
    loop(NP - 1, send_wd)

    arrived(x_all.at[pl.ds(0, NZ - 1)], X)
    arrived(wgu.at[:, half_g], WGUF)
    x = x_all[...].reshape(ROWS, COLS)
    def send_h(k):
        m = plane(k + 1)
        h_out[m] = jnp.dot(x, wgu[m], preferred_element_type=F32).astype(BF16)
        put(h_out.at[m], h_in.at[n], H, c, z * NP + m)
    loop(NP - 1, send_h)
    h_out[n] = jnp.dot(x, wgu[n], preferred_element_type=F32).astype(BF16)
    keep(h_out.at[n], h_in.at[n], H)

    arrived(wd.at[:, half_d], WD)
    put(wd.at[:, half_d], wd.at[:, half_d], WDF, 1 - c, h)

    arrived(rs_all.at[pl.ds(0, NZ - 1)], RS)
    tiles = rs_all[...].reshape(ROWS, 128)
    lanes = lax.broadcasted_iota(jnp.int32, (ROWS, 128), 1)
    scale = jnp.sum(jnp.where(lanes == 8, tiles, 0.0), axis=-1, keepdims=True)
    gate_of = jnp.sum(jnp.where(lanes == z, tiles, 0.0), axis=-1, keepdims=True)

    arrived(h_in, H)
    products = h_in[0].astype(F32)
    for i in range(1, NP):
        products = products + h_in[i].astype(F32)
    products = products * scale
    gated = products[:, :UNITS]
    hid_own[...] = (gated * jax.nn.sigmoid(gated) * products[:, UNITS:]).astype(BF16)
    keep(hid_own, hid_all.at[n], HID)
    def send_hid(k):
        put(hid_own, hid_all.at[n], HID, c, z * NP + plane(k + 1))
    loop(NP - 1, send_hid)

    arrived(wd.at[:, half_d], WDF)
    arrived(hid_all, HID)
    hidden = jnp.concatenate([hid_all[i] for i in range(NP)], axis=1)
    expert = jnp.dot(hidden, wd[...].reshape(NP * UNITS, COLS), preferred_element_type=F32)
    o_out[...] = (expert * gate_of).astype(BF16).reshape(NZ, CHUNK, COLS)
    keep(o_out.at[z], o_in.at[z], O)
    def send_o(k):
        m = depth(k + 1)
        put(o_out.at[m], o_in.at[z], O, c, m * NP + n)
    loop(NZ - 1, send_o)

    arrived(o_in, O)
    mixture = o_in[0].astype(F32)
    for i in range(1, NZ):
        mixture = mixture + o_in[i].astype(F32)
    mix_out[...] = mixture.reshape(NY, OWN, COLS).astype(BF16)
    home(1, mix_out, mix_in, MIX)

    def finish(landing, phase):
        arrived(landing, phase)
        for i in range(NP):
            out_ref[:, i * COLS:(i + 1) * COLS] = landing[i]

    @pl.when(c == 0)
    def _():
        finish(stream_in, STREAM)

    @pl.when(c == 1)
    def _():
        finish(mix_in, MIX)

    gone(qbuf, Q)
    gone(resbuf, RES)
    gone(selbuf, SEL)
    gone(lat_in, LATS)
    part = pl.ds(0, NP - 1)
    gone(wo.at[part, half_o], WO)
    gone(wo.at[:, half_o], WOF)
    gone(head_all.at[part], HEAD)
    gone(c_in.at[part], C)
    gone(ssq_in.at[part], SSQ)
    gone(rs_all.at[part], RS)
    gone(x_all.at[part], X)
    gone(wgu.at[part, half_g, pl.ds(0, 128)], WG)
    gone(wgu.at[part, half_g, pl.ds(128, 128)], WU)
    gone(wgu.at[:, half_g], WGUF)
    gone(wd.at[part, half_d], WD)
    gone(wd.at[:, half_d], WDF)
    gone(h_in.at[part], H)
    gone(hid_all.at[part], HID)
    gone(o_in.at[part], O)

    def gone_home(core, src, phase):
        own = (c == core) & (xl == c)
        @pl.when(own)
        def _():
            gone(src.at[pl.ds(0, NY - 1)], phase)
        @pl.when(jnp.logical_not(own))
        def _():
            gone(src, phase)

    gone_home(0, stream_out, STREAM)
    gone_home(1, mix_out, MIX)


def per_device(
    queries, cache_pool, block_table, cache_len, w_uv, w_out, residual, norm_gain,
    expert_ids, expert_gates, w_gate, w_up, w_down,
):
    hbm = pl.BlockSpec(memory_space=pl.ANY)
    vmem = pl.BlockSpec(memory_space=pltpu.VMEM)
    smem = pl.BlockSpec(memory_space=pltpu.SMEM)
    shapes = [
        ((16, 64, KW), BF16),
        ((LAT, VH), BF16),
        ((1, COLS), F32),
        ((NH, OWN, KW), BF16),
        ((NH, OWN, LAT), BF16),
        ((NH, OWN, LAT), BF16),
        ((OWN, 128), F32),
        ((NY, OWN, COLS), BF16),
        ((NY, OWN, 128), F32),
        ((NP, VH, COLS), BF16),
        ((NP, COLS, 2 * UNITS), BF16),
        ((NP, UNITS, COLS), BF16),
        ((ROWS, VH), BF16),
        ((NP, ROWS, VH), BF16),
        ((NZ, CHUNK, COLS), BF16),
        ((NZ, CHUNK, COLS), BF16),
        ((NY, OWN, COLS), BF16),
        ((NP, OWN, COLS), BF16),
        ((CHUNK, 128), F32),
        ((NP, CHUNK, 128), F32),
        ((NZ, CHUNK, 128), F32),
        ((NZ, CHUNK, COLS), BF16),
        ((NP, ROWS, 2 * UNITS), BF16),
        ((NP, ROWS, 2 * UNITS), BF16),
        ((ROWS, UNITS), BF16),
        ((NP, ROWS, UNITS), BF16),
        ((NZ, CHUNK, COLS), BF16),
        ((NZ, CHUNK, COLS), BF16),
        ((NY, OWN, COLS), BF16),
        ((NP, OWN, COLS), BF16),
    ]
    result = pl.pallas_call(
        kernel,
        out_shape=jax.ShapeDtypeStruct((OWN, D), BF16),
        in_specs=[hbm, hbm, vmem, smem, hbm, hbm, hbm, hbm, vmem, vmem, hbm, hbm, hbm],
        out_specs=vmem,
        scratch_shapes=[pltpu.VMEM(shape, dtype) for shape, dtype in shapes] + [
            pltpu.SemaphoreType.DMA((3,)),
            pltpu.SemaphoreType.DMA((21,)),
            pltpu.SemaphoreType.DMA((21,)),
        ],
        compiler_params=pltpu.CompilerParams(
            has_side_effects=True, vmem_limit_bytes=44 * 1024 * 1024),
        cost_estimate=pl.CostEstimate(
            flops=4_000_000_000, bytes_accessed=16_000_000, transcendentals=400_000),
        name="layer",
    )(
        queries.reshape(64, OWN, KW), cache_pool[0], block_table[0], cache_len[0],
        w_uv[0], w_out[0], residual[0], norm_gain.reshape(1, D),
        expert_ids[0], expert_gates[0], w_gate[0], w_up[0], w_down[0],
    )
    return result[None, None]


def solution(mesh):
    in_specs = (
        P("sub", None, "head", None),
        P("sub", "head", None, None),
        P("sub", "head", None),
        P("sub", "head"),
        P("head", None, None),
        P("head", None, None),
        P("sub", "head", None),
        P(),
        P("sub", "head", None),
        P("sub", "head", None),
        P("head", None, None),
        P("head", None, None),
        P("head", None, None),
    )
    out_specs = P("side", "sub", "head", None)
    return jax.shard_map(
        per_device, mesh=mesh, in_specs=in_specs, out_specs=out_specs, check_vma=False
    )
```

time: 799 us -> 152 us (0.19)
  waiting for transfers between devices: 670 us -> 0 us
  Pallas kernels: 0 us -> 135 us
  starting transfers between devices: 39.2 us -> 0 us
  matrix products: 31.6 us -> 0 us
  blocking collectives: 19.9 us -> 0 us
  between operations: 13.6 us -> 0.03 us
  other arithmetic: 8.07 us -> 0 us
    all_to_all x3 -> x0, waiting for transfers between devices: 325 us -> none  [the longest x1 161 us: per_device(): lax.all_to_all(outgoing, 'head', split_axis=0, concat_axis=0, tiled=True)]
    reduce_scatter x1 -> x0, waiting for transfers between devices: 299 us -> none  [per_device(): lax.psum_scatter(jnp.dot(head_out, w_out[0], preferred_element_type=jnp.f...]
    pallas_call x0 -> x1, Pallas kernels: none -> 135 us  [per_device(): pl.pallas_call(kernel, out_shape=jax.ShapeDtypeStruct((OWN, D), BF16), in...]
    ppermute x1 -> x0, waiting for transfers between devices: 47.2 us -> none  [passed_along(): return lax.ppermute(block, axis, route)]
    all_to_all x3 -> x0, starting transfers between devices: 37.9 us -> none  [the longest x1 15.3 us: per_device(): lax.all_to_all(outgoing, 'head', split_axis=0, concat_axis=0, tiled=True)]
    dot_general x5 -> x0, matrix products: 31.6 us -> none  [the longest x1 14.9 us: expert_ffn(): jnp.einsum('siu,ud->sid', hidden, w_down[0], preferred_element_type=jnp.f...]
    all_to_all x1 -> x0, blocking collectives: 19.9 us -> none  [per_device(): lax.all_to_all(own_latents, 'head', split_axis=1, concat_axis=0, tiled=True)]
  transfers between devices with their start and end apart: 5 -> 0, of which waited for: 5 -> 0; matrix products, arithmetic and copies ran while one was open for 0% -> 0% of each run, Pallas kernels for 0% -> 0%
where the time goes in v1:
time: 152 us; the launch traced here: 150 us
  Pallas kernels  135 us (89%)
  local copies, waits for them, and re-layouts  14.8 us (10%)
    pallas_call x1, Pallas kernels, per_device(): pl.pallas_call(kernel, out_shape=jax.ShapeDtypeStruct((OWN, D), BF16), in...  135 us
    unnamed x20, local copies, waits for them, and re-layouts  12.5 us

profile of v1, /device:TPU:25, one launch (start us, length us, event | category | flops | bytes accessed | tf_op | source)
XLA Modules:
  0.0 149.6 jit_solution(14545241177438802940)
XLA Ops:
  0.0 0.8 copy.15.tab_ref
  0.8 0.8 copy.16.ids_ref
  1.5 0.8 copy.17.gates_ref
  2.3 1.4 copy.14
  3.6 0.0 copy-start
  3.6 1.5 copy-done
  5.1 0.0 copy-start.1
  5.1 1.5 %copy-done.1 = bf16[1,7168,128]{2,1,0:T(8,128)(2,1)S(1)} copy-done((bf16[1,7168,128]{2,1,0:T(8,128)(2,1)S(1)}, bf16[1,7168,128]{2,1,0:T(8,128)(2,1)}, u32[]{:S(2)}) %copy-start.1) | copy-done | bytes 1835032
  6.6 0.0 copy-start.2
  6.6 1.5 %copy-done.2 = bf16[1,7168,128]{2,1,0:T(8,128)(2,1)S(1)} copy-done((bf16[1,7168,128]{2,1,0:T(8,128)(2,1)S(1)}, bf16[1,7168,128]{2,1,0:T(8,128)(2,1)}, u32[]{:S(2)}) %copy-start.2) | copy-done | bytes 1835032
  8.1 0.0 copy-start.3
  8.1 1.5 %copy-done.3 = bf16[1,128,7168]{2,1,0:T(8,128)(2,1)S(1)} copy-done((bf16[1,128,7168]{2,1,0:T(8,128)(2,1)S(1)}, bf16[1,128,7168]{2,1,0:T(8,128)(2,1)}, u32[]{:S(2)}) %copy-start.3) | copy-done | bytes 1835032
  9.6 0.0 copy-start.4
  9.6 1.3 copy-done.4
  10.9 0.0 copy-start.5
  10.9 0.9 copy-done.5
  11.8 0.0 copy-start.6
  11.9 0.9 copy-done.6
  12.7 0.0 copy-start.7
  12.8 0.7 copy-done.7
  13.5 0.0 copy-start.8
  13.5 0.7 copy-done.8
  14.2 134.8 %layer.1 = bf16[8,7168]{1,0:T(8,128)(2,1)S(1)} custom-call(bf16[64,8,576]{2,1,0:T(8,128)(2,1)S(1)} %bitcast.14, bf16[16,64,576]{2,1,0:T(8,128)(2,1)S(1)} %bitcast.20, s32[8,2]{1,0:T(8,128)S(1)} %copy.15.tab_ref, s32[8]{0:T(128)S(1)} %bitcast.24, bf16[512,128]{1,0:T(8,128)(2,1)S(1)} %bitcast.21, bf16[128,7168]{1,0:T(8,128)(2,1)S(1)} %bitcast.16, ...), custom_call_target="tpu_custom_call" | custom-call | flops 4000000000 | bytes 16000000 | tf_op jit(solution)/shard_map/layer/pallas_call | solution.py:366
  149.0 0.6 copy.19
Async XLA Ops:
  3.6 1.5 %copy-start = (bf16[1,128,7168]{2,1,0:T(8,128)(2,1)S(1)}, bf16[1,128,7168]{2,1,0:T(8,128)(2,1)}, u32[]{:S(2)}) copy-start(bf16[1,128,7168]{2,1,0:T(8,128)(2,1)} %param.18) | copy-start | bytes 5505028
  5.1 1.5 %copy-start.1 = (bf16[1,7168,128]{2,1,0:T(8,128)(2,1)S(1)}, bf16[1,7168,128]{2,1,0:T(8,128)(2,1)}, u32[]{:S(2)}) copy-start(bf16[1,7168,128]{2,1,0:T(8,128)(2,1)} %param.23) | copy-start | bytes 5505028
  6.6 1.5 %copy-start.2 = (bf16[1,7168,128]{2,1,0:T(8,128)(2,1)S(1)}, bf16[1,7168,128]{2,1,0:T(8,128)(2,1)}, u32[]{:S(2)}) copy-start(bf16[1,7168,128]{2,1,0:T(8,128)(2,1)} %param.24) | copy-start | bytes 5505028
  8.1 1.5 %copy-start.3 = (bf16[1,128,7168]{2,1,0:T(8,128)(2,1)S(1)}, bf16[1,128,7168]{2,1,0:T(8,128)(2,1)}, u32[]{:S(2)}) copy-start(bf16[1,128,7168]{2,1,0:T(8,128)(2,1)} %param.25) | copy-start | bytes 5505028
  9.6 1.3 copy-start.4
  10.9 0.9 copy-start.5
  11.8 0.9 copy-start.6
  12.7 0.7 copy-start.7
  13.5 0.7 copy-start.8

commit v2 on v1

v2 whole, which is shorter than its diff:
```python
import jax
import jax.numpy as jnp
from jax import lax
from jax.experimental import pallas as pl
from jax.experimental.pallas import tpu as pltpu
from jax.sharding import PartitionSpec as P

D = 7168
LAT = 512
KW = 576
VH = 128
UNITS = 128
EPS = 1e-6
SCALE = 192 ** (-0.5)

NZ = 8
NP = 8
NY = 4
OWN = 8
COLS = D // NP
CHUNK = NY * OWN
ROWS = NZ * CHUNK
NH = NZ * NY
HB = 2
PART = ROWS // HB
STRIP = CHUNK // HB
MEET = 2 * NH + 2 * NP - 1 + NZ - 1
F32 = jnp.float32
BF16 = jnp.bfloat16


NAMES = (
    ["Q", "RES", "SEL", "LATS", "WO", "WOF", "WG", "WGF", "WU", "WUF", "WD", "WDF", "STREAM", "MIX"]
    + [name + str(b) for name in ("HEAD", "C", "SSQ", "RS", "X", "H", "HID", "O") for b in range(HB)]
)
PHASE = {name: i for i, name in enumerate(NAMES)}


def kernel(
    q_ref, pool_ref, tab_ref, len_ref, wuv_ref, wout_ref, res_ref, gain_ref,
    ids_ref, gates_ref, wg_ref, wu_ref, wd_ref,
    out_ref,
    qcols, qrows, pool, wuv, gain, qbuf, lat_out, lat_in, sel, resbuf, selbuf,
    wo, wgu, wd, head_own, head_all, c_out, c_in,
    stream_out, stream_in, ssq_own, ssq_in, rs_all, x_all,
    h_out, h_in, hid_own, hid_all, o_out, o_in, mix_out, mix_in,
    load, send, recv,
):
    c = lax.axis_index("side")
    h = lax.axis_index("head")
    sub = lax.axis_index("sub")
    z, n = h // NP, h % NP
    xl, y = n // NY, n % NY
    spot = z * NY + y

    def device(core, head):
        return (core, head, sub)

    def put(src, dst, phase, core, head):
        pltpu.make_async_remote_copy(
            src_ref=src, dst_ref=dst,
            send_sem=send.at[PHASE[phase]], recv_sem=recv.at[PHASE[phase]],
            device_id=device(core, head), device_id_type=pl.DeviceIdType.MESH,
        ).start()

    def keep(src, dst, phase):
        pltpu.make_async_copy(src, dst, recv.at[PHASE[phase]]).start()

    def arrived(ref, phase):
        with jax.named_scope("w_" + phase):
            pltpu.make_async_copy(ref, ref, recv.at[PHASE[phase]]).wait()

    def gone(ref, phase):
        pltpu.make_async_copy(ref, ref, send.at[PHASE[phase]]).wait()

    def loop(count, body):
        def step(k, carry):
            body(k)
            return carry
        lax.fori_loop(0, count, step, 0)

    def plane(k):
        return (n + k) % NP

    def depth(k):
        return (z + k) % NZ

    def cols(m):
        return pl.ds(pl.multiple_of(m * COLS, 128), COLS)

    loads = [
        pltpu.make_async_copy(q_ref, qcols, load.at[0]),
        pltpu.make_async_copy(pool_ref, pool, load.at[1]),
        pltpu.make_async_copy(wuv_ref, wuv, load.at[2]),
        pltpu.make_async_copy(gain_ref.at[:, cols(n)], gain, load.at[3]),
    ]
    for copy in loads:
        copy.start()

    barrier = pltpu.get_barrier_semaphore()

    def greet(core, head):
        pl.semaphore_signal(
            barrier, inc=1, device_id=device(core, head), device_id_type=pl.DeviceIdType.MESH)

    def greet_far(k):
        m = (k + spot) % NH
        greet(1 - xl, (m // NY) * NP + c * NY + m % NY)
        greet(xl, (m // NY) * NP + (1 - c) * NY + m % NY)
    loop(NH, greet_far)

    def greet_plane(k):
        m = (c * NP + n + k + 1) % (2 * NP)
        greet(m // NP, z * NP + m % NP)
    loop(2 * NP - 1, greet_plane)

    def greet_depth(k):
        greet(c, depth(k + 1) * NP + n)
    loop(NZ - 1, greet_depth)

    loads[0].wait()
    for i in range(0, KW, 128):
        wide = min(128, KW - i)
        turned = jnp.transpose(qcols[i:i + wide, :].astype(F32))
        qrows[:, :, i:i + wide] = turned.reshape(64, OWN, wide).astype(BF16)

    lane = lax.broadcasted_iota(jnp.int32, (OWN, 128), 1)
    line = lax.broadcasted_iota(jnp.int32, (OWN, 128), 0)
    picked = jnp.zeros((OWN, 128), F32)
    for r in range(OWN):
        for k in range(ids_ref.shape[0]):
            picked = picked + jnp.where((line == r) & (lane == ids_ref[k, r]), gates_ref[k, r], 0.0)
    sel[...] = picked

    row = lax.broadcasted_iota(jnp.int32, (OWN, 1024), 0)
    place = lax.broadcasted_iota(jnp.int32, (OWN, 1024), 1)
    block, offset = place // 64, place % 64
    bias = jnp.full((OWN, 1024), -1e30, F32)
    for r in range(OWN):
        seen = ((block == tab_ref[0, r]) & (offset < len_ref[0, r])) | (
            (block == tab_ref[1, r]) & (offset + 64 < len_ref[0, r]))
        bias = jnp.where((row == r) & seen, 0.0, bias)

    with jax.named_scope("w_barrier"):
        pl.semaphore_wait(barrier, MEET)

    def send_query(k):
        m = (k + spot) % NH
        owner = (m // NY) * NP + c * NY + m % NY
        put(qrows.at[owner], qbuf.at[spot], "Q", 1 - xl, owner)
    loop(NH, send_query)

    def send_residual(k):
        m = (1 - c) * NY + (y + k) % NY
        put(res_ref.at[:, cols(m)], resbuf.at[y], "RES", xl, z * NP + m)
        put(sel, selbuf.at[y], "SEL", xl, z * NP + m)
    loop(NY, send_residual)

    half = pl.ds(pl.multiple_of(c * 64, 64), 64)
    half_g = pl.ds(pl.multiple_of(c * (COLS // 2), COLS // 2), COLS // 2)
    left, right = pl.ds(0, UNITS), pl.ds(UNITS, UNITS)

    def depth_rows(m):
        return pl.ds(pl.multiple_of(m * COLS + c * (COLS // 2), COLS // 2), COLS // 2)

    def share(source, landing, phase):
        keep(source(n), landing, phase)
        def step(k):
            m = plane(k + 1)
            put(source(m), landing, phase, c, z * NP + m)
        loop(NP - 1, step)

    share(lambda m: wout_ref.at[half, cols(m)], wo.at[n, half], "WO")

    loads[1].wait()
    arrived(qbuf, "Q")
    queries = qbuf[...].astype(F32).reshape(NH * OWN, KW).astype(BF16)
    keys = pool[...].reshape(1024, KW)
    scores = lax.dot_general(
        queries, keys, (((1,), (1,)), ((), ())), preferred_element_type=F32)
    scores = scores.reshape(NH, OWN, 1024) * SCALE + bias[None]
    scores = scores.reshape(NH * OWN, 1024)
    peak = jnp.max(scores, axis=-1, keepdims=True)
    raw = jnp.exp(scores - peak)
    total = jnp.sum(raw, axis=-1, keepdims=True)
    latents = jnp.dot(raw.astype(BF16), keys[:, :LAT], preferred_element_type=F32) / total
    lat_out[...] = latents.reshape(NH, OWN, LAT).astype(BF16)

    def send_latent(k):
        m = (k + spot) % NH
        put(lat_out.at[m], lat_in.at[y // 2, z, y % 2], "LATS",
            xl, (m // NY) * NP + (1 - c) * NY + m % NY)
    loop(NH, send_latent)

    share(lambda m: wg_ref.at[depth_rows(m)], wgu.at[n, half_g, left], "WG")

    arrived(wo.at[:, half], "WO")
    put(wo.at[:, half], wo.at[:, half], "WOF", 1 - c, h)

    loads[2].wait()
    arrived(lat_in, "LATS")
    for b in range(HB):
        rows = lat_in[b].astype(F32).reshape(PART, LAT).astype(BF16)
        head_own[b] = jnp.dot(rows, wuv[...], preferred_element_type=F32).astype(BF16)
        keep(head_own.at[b], head_all.at[b, n], f"HEAD{b}")
        def send_head(k):
            put(head_own.at[b], head_all.at[b, n], f"HEAD{b}", c, z * NP + plane(k + 1))
        loop(NP - 1, send_head)

    arrived(wo.at[:, half], "WOF")
    for b in range(HB):
        arrived(head_all.at[b], f"HEAD{b}")
        heads = jnp.concatenate([head_all[b, i] for i in range(NP)], axis=1)
        partial = jnp.dot(heads, wo[...].reshape(NP * VH, COLS), preferred_element_type=F32)
        c_out[b] = partial.astype(BF16).reshape(NZ, STRIP, COLS)
        keep(c_out.at[b, z], c_in.at[b, z], f"C{b}")
        def send_c(k):
            m = depth(k + 1)
            put(c_out.at[b, m], c_in.at[b, z], f"C{b}", c, m * NP + n)
        loop(NZ - 1, send_c)

    share(lambda m: wu_ref.at[depth_rows(m)], wgu.at[n, half_g, right], "WU")
    share(lambda m: wd_ref.at[half, cols(m)], wd.at[n, half], "WD")
    arrived(wgu.at[:, half_g, left], "WG")
    put(wgu.at[:, half_g, left], wgu.at[:, half_g, left], "WGF", 1 - c, h)

    def home(core, src, landing, phase, k):
        own = (c == core) & (xl == c) & (y == k)
        @pl.when(own)
        def _():
            keep(src.at[k], landing.at[n], phase)
        @pl.when(jnp.logical_not(own))
        def _():
            put(src.at[k], landing.at[n], phase, core, z * NP + c * NY + k)

    arrived(resbuf, "RES")
    arrived(selbuf, "SEL")
    loads[3].wait()
    for b in range(HB):
        pair = slice(2 * b, 2 * b + 2)
        arrived(c_in.at[b], f"C{b}")
        attended = c_in[b, 0].astype(F32)
        for i in range(1, NZ):
            attended = attended + c_in[b, i].astype(F32)
        residual = resbuf[pair].astype(F32).reshape(STRIP, COLS)
        stream = (residual + attended).astype(BF16).astype(F32)
        x_all[b, z] = (stream * gain[...]).astype(BF16)
        def send_x(k):
            put(x_all.at[b, z], x_all.at[b, z], f"X{b}", c, depth(k + 1) * NP + n)
        loop(NZ - 1, send_x)

        squares = jnp.sum(stream * stream, axis=-1, keepdims=True)
        ssq_own[b] = jnp.broadcast_to(squares, (STRIP, 128))
        keep(ssq_own.at[b], ssq_in.at[b, n], f"SSQ{b}")
        def send_ssq(k):
            put(ssq_own.at[b], ssq_in.at[b, n], f"SSQ{b}", c, z * NP + plane(k + 1))
        loop(NP - 1, send_ssq)

        stream_out[pair] = stream.reshape(2, OWN, COLS).astype(BF16)
        home(0, stream_out, stream_in, "STREAM", 2 * b)
        home(0, stream_out, stream_in, "STREAM", 2 * b + 1)

    for b in range(HB):
        arrived(ssq_in.at[b], f"SSQ{b}")
        square = ssq_in[b, 0]
        for i in range(1, NP):
            square = square + ssq_in[b, i]
        scale = lax.rsqrt(square * (1.0 / D) + EPS)
        wide = lax.broadcasted_iota(jnp.int32, (STRIP, 128), 1)
        chosen = selbuf[2 * b:2 * b + 2].reshape(STRIP, 128)
        rs_all[b, z] = jnp.where(wide < 8, chosen, scale)
        def send_rs(k):
            put(rs_all.at[b, z], rs_all.at[b, z], f"RS{b}", c, depth(k + 1) * NP + n)
        loop(NZ - 1, send_rs)

    arrived(wgu.at[:, half_g, right], "WU")
    put(wgu.at[:, half_g, right], wgu.at[:, half_g, right], "WUF", 1 - c, h)

    arrived(wgu.at[:, half_g, left], "WGF")
    arrived(wgu.at[:, half_g, right], "WUF")
    others = pl.ds(0, NP - 1)
    for b in range(HB):
        arrived(x_all.at[b, others], f"X{b}")
        x = x_all[b].reshape(PART, COLS)
        def send_h(k):
            m = plane(k + 1)
            h_out[b, m] = jnp.dot(x, wgu[m], preferred_element_type=F32).astype(BF16)
            put(h_out.at[b, m], h_in.at[b, n], f"H{b}", c, z * NP + m)
        loop(NP - 1, send_h)
        h_out[b, n] = jnp.dot(x, wgu[n], preferred_element_type=F32).astype(BF16)
        keep(h_out.at[b, n], h_in.at[b, n], f"H{b}")

    arrived(wd.at[:, half], "WD")
    put(wd.at[:, half], wd.at[:, half], "WDF", 1 - c, h)

    lanes = lax.broadcasted_iota(jnp.int32, (PART, 128), 1)
    gate_of = []
    for b in range(HB):
        arrived(rs_all.at[b, others], f"RS{b}")
        tiles = rs_all[b].reshape(PART, 128)
        scale = jnp.sum(jnp.where(lanes == 8, tiles, 0.0), axis=-1, keepdims=True)
        gate_of.append(jnp.sum(jnp.where(lanes == z, tiles, 0.0), axis=-1, keepdims=True))

        arrived(h_in.at[b], f"H{b}")
        products = h_in[b, 0].astype(F32)
        for i in range(1, NP):
            products = products + h_in[b, i].astype(F32)
        products = products * scale
        gated = products[:, :UNITS]
        hid_own[b] = (gated * jax.nn.sigmoid(gated) * products[:, UNITS:]).astype(BF16)
        keep(hid_own.at[b], hid_all.at[b, n], f"HID{b}")
        def send_hid(k):
            put(hid_own.at[b], hid_all.at[b, n], f"HID{b}", c, z * NP + plane(k + 1))
        loop(NP - 1, send_hid)

    arrived(wd.at[:, half], "WDF")
    for b in range(HB):
        arrived(hid_all.at[b], f"HID{b}")
        hidden = jnp.concatenate([hid_all[b, i] for i in range(NP)], axis=1)
        expert = jnp.dot(hidden, wd[...].reshape(NP * UNITS, COLS), preferred_element_type=F32)
        o_out[b] = (expert * gate_of[b]).astype(BF16).reshape(NZ, STRIP, COLS)
        keep(o_out.at[b, z], o_in.at[b, z], f"O{b}")
        def send_o(k):
            m = depth(k + 1)
            put(o_out.at[b, m], o_in.at[b, z], f"O{b}", c, m * NP + n)
        loop(NZ - 1, send_o)

    for b in range(HB):
        arrived(o_in.at[b], f"O{b}")
        mixture = o_in[b, 0].astype(F32)
        for i in range(1, NZ):
            mixture = mixture + o_in[b, i].astype(F32)
        mix_out[2 * b:2 * b + 2] = mixture.reshape(2, OWN, COLS).astype(BF16)
        home(1, mix_out, mix_in, "MIX", 2 * b)
        home(1, mix_out, mix_in, "MIX", 2 * b + 1)

    def finish(landing, phase):
        arrived(landing, phase)
        for i in range(NP):
            out_ref[:, i * COLS:(i + 1) * COLS] = landing[i]

    @pl.when(c == 0)
    def _():
        finish(stream_in, "STREAM")

    @pl.when(c == 1)
    def _():
        finish(mix_in, "MIX")

    gone(qbuf, "Q")
    gone(resbuf, "RES")
    gone(selbuf, "SEL")
    gone(lat_in, "LATS")
    gone(wo.at[others, half], "WO")
    gone(wo.at[:, half], "WOF")
    gone(wgu.at[others, half_g, left], "WG")
    gone(wgu.at[:, half_g, left], "WGF")
    gone(wgu.at[others, half_g, right], "WU")
    gone(wgu.at[:, half_g, right], "WUF")
    gone(wd.at[others, half], "WD")
    gone(wd.at[:, half], "WDF")
    for b in range(HB):
        gone(head_all.at[b, others], f"HEAD{b}")
        gone(c_in.at[b, others], f"C{b}")
        gone(ssq_in.at[b, others], f"SSQ{b}")
        gone(rs_all.at[b, others], f"RS{b}")
        gone(x_all.at[b, others], f"X{b}")
        gone(h_in.at[b, others], f"H{b}")
        gone(hid_all.at[b, others], f"HID{b}")
        gone(o_in.at[b, others], f"O{b}")

    def gone_home(core, src, phase):
        own = (c == core) & (xl == c)
        @pl.when(own)
        def _():
            gone(src.at[pl.ds(0, NY - 1)], phase)
        @pl.when(jnp.logical_not(own))
        def _():
            gone(src, phase)

    gone_home(0, stream_out, "STREAM")
    gone_home(1, mix_out, "MIX")


def per_device(
    queries, cache_pool, block_table, cache_len, w_uv, w_out, residual, norm_gain,
    expert_ids, expert_gates, w_gate, w_up, w_down,
):
    hbm = pl.BlockSpec(memory_space=pl.ANY)
    smem = pl.BlockSpec(memory_space=pltpu.SMEM)
    shapes = [
        ((KW, 512), BF16),
        ((64, OWN, KW), BF16),
        ((16, 64, KW), BF16),
        ((LAT, VH), BF16),
        ((1, COLS), F32),
        ((NH, OWN, KW), BF16),
        ((NH, OWN, LAT), BF16),
        ((HB, NZ, 2, OWN, LAT), BF16),
        ((OWN, 128), F32),
        ((NY, OWN, COLS), BF16),
        ((NY, OWN, 128), F32),
        ((NP, VH, COLS), BF16),
        ((NP, COLS, 2 * UNITS), BF16),
        ((NP, UNITS, COLS), BF16),
        ((HB, PART, VH), BF16),
        ((HB, NP, PART, VH), BF16),
        ((HB, NZ, STRIP, COLS), BF16),
        ((HB, NZ, STRIP, COLS), BF16),
        ((NY, OWN, COLS), BF16),
        ((NP, OWN, COLS), BF16),
        ((HB, STRIP, 128), F32),
        ((HB, NP, STRIP, 128), F32),
        ((HB, NZ, STRIP, 128), F32),
        ((HB, NZ, STRIP, COLS), BF16),
        ((HB, NP, PART, 2 * UNITS), BF16),
        ((HB, NP, PART, 2 * UNITS), BF16),
        ((HB, PART, UNITS), BF16),
        ((HB, NP, PART, UNITS), BF16),
        ((HB, NZ, STRIP, COLS), BF16),
        ((HB, NZ, STRIP, COLS), BF16),
        ((NY, OWN, COLS), BF16),
        ((NP, OWN, COLS), BF16),
    ]
    result = pl.pallas_call(
        kernel,
        out_shape=jax.ShapeDtypeStruct((OWN, D), BF16),
        in_specs=[hbm, hbm, smem, smem, hbm, hbm, hbm, hbm, smem, smem, hbm, hbm, hbm],
        out_specs=pl.BlockSpec(memory_space=pltpu.VMEM),
        scratch_shapes=[pltpu.VMEM(shape, dtype) for shape, dtype in shapes] + [
            pltpu.SemaphoreType.DMA((4,)),
            pltpu.SemaphoreType.DMA((len(NAMES),)),
            pltpu.SemaphoreType.DMA((len(NAMES),)),
        ],
        compiler_params=pltpu.CompilerParams(
            collective_id=0, has_side_effects=True, vmem_limit_bytes=60 * 1024 * 1024),
        cost_estimate=pl.CostEstimate(
            flops=4_000_000_000, bytes_accessed=16_000_000, transcendentals=400_000),
        name="layer",
    )(
        queries[0, :, 0, :].T, cache_pool[0], block_table[0].T, cache_len,
        w_uv[0], w_out[0], residual[0], norm_gain.reshape(1, D),
        expert_ids[0].T, expert_gates[0].T, w_gate[0], w_up[0], w_down[0],
    )
    return result[None, None]


def solution(mesh):
    in_specs = (
        P("sub", None, "head", None),
        P("sub", "head", None, None),
        P("sub", "head", None),
        P("sub", "head"),
        P("head", None, None),
        P("head", None, None),
        P("sub", "head", None),
        P(),
        P("sub", "head", None),
        P("sub", "head", None),
        P("head", None, None),
        P("head", None, None),
        P("head", None, None),
    )
    out_specs = P("side", "sub", "head", None)
    return jax.shard_map(
        per_device, mesh=mesh, in_specs=in_specs, out_specs=out_specs, check_vma=False
    )
```

time: 152 us -> 118 us (0.78)
  Pallas kernels: 135 us -> 114 us
  local copies, waits for them, and re-layouts: 14.8 us -> 1.55 us
    pallas_call x1, Pallas kernels: 135 us -> 114 us  [per_device(): pl.pallas_call(kernel, out_shape=jax.ShapeDtypeStruct((OWN, D), BF16), in...]
    unnamed x20 -> x1, local copies, waits for them, and re-layouts: 12.5 us -> 1.55 us
    squeeze x3 -> x0, local copies, waits for them, and re-layouts: 2.26 us -> none  [the longest x1 0.76 us: per_device(): expert_ids[0]]
where the time goes in v2:
time: 118 us; the launch traced here: 116 us
  Pallas kernels  114 us (97%)
  local copies, waits for them, and re-layouts  1.55 us (1%)
    pallas_call x1, Pallas kernels, per_device(): pl.pallas_call(kernel, out_shape=jax.ShapeDtypeStruct((OWN, D), BF16), in...  114 us

profile of v2, /device:TPU:25, one launch (start us, length us, event | category | flops | bytes accessed | tf_op | source)
XLA Modules:
  0.0 115.6 jit_solution(4122525769133099390)
XLA Ops:
  0.0 114.0 %layer.1 = bf16[8,7168]{1,0:T(8,128)(2,1)} custom-call(bf16[576,512]{1,0:T(8,128)(2,1)} %bitcast.27, bf16[16,64,576]{2,1,0:T(8,128)(2,1)} %bitcast.26, s32[2,8]{1,0:T(2,128)} %bitcast.33, s32[1,8]{1,0:T(1,128)} %len_ref.1, bf16[512,128]{1,0:T(8,128)(2,1)} %bitcast.28, bf16[128,7168]{1,0:T(8,128)(2,1)} %bitcast.22, bf16[8,7168]{1,0:T(8,128)(2,1)} %bitcast.29, ...), custom_call_target="tpu_custom_call" | custom-call | flops 4000000000 | bytes 16000000 | tf_op jit(solution)/shard_map/layer/pallas_call | solution.py:425
  114.1 1.6 %copy.15 = bf16[1,1,8,7168]{3,2,1,0:T(8,128)(2,1)} copy(bf16[1,1,8,7168]{3,2,1,0:T(8,128)(2,1)} %bitcast.21) | data formatting | bytes 229376

commit v3 on v2

--- a/solution.py
+++ b/solution.py
@@ -31,7 +31,7 @@
 
 NAMES = (
     ["Q", "RES", "SEL", "LATS", "WO", "WOF", "WG", "WGF", "WU", "WUF", "WD", "WDF", "STREAM", "MIX"]
-    + [name + str(b) for name in ("HEAD", "C", "SSQ", "RS", "X", "H", "HID", "O") for b in range(HB)]
+    + [name + str(b) for name in ("HEAD", "C", "SIDE", "SQ", "X", "H", "HID", "O") for b in range(HB)]
 )
 PHASE = {name: i for i, name in enumerate(NAMES)}
 
@@ -42,7 +42,7 @@
     out_ref,
     qcols, qrows, pool, wuv, gain, qbuf, lat_out, lat_in, sel, resbuf, selbuf,
     wo, wgu, wd, head_own, head_all, c_out, c_in,
-    stream_out, stream_in, ssq_own, ssq_in, rs_all, x_all,
+    stream_out, stream_in, side_all, sq_own, sq_in, x_all,
     h_out, h_in, hid_own, hid_all, o_out, o_in, mix_out, mix_in,
     load, send, recv,
 ):
@@ -79,11 +79,17 @@
             return carry
         lax.fori_loop(0, count, step, 0)
 
+    def around(k, me, size):
+        far = (k + 1) // 2
+        return (me + size + far * (2 * (k % 2) - 1)) % size
+
+    def depth(k):
+        return around(k + 1, z, NZ)
+
     def plane(k):
-        return (n + k) % NP
-
-    def depth(k):
-        return (z + k) % NZ
+        turn = jnp.where(k < 4, 1 + 2 * (k % 2), jnp.where(k == 4, 0, 2))
+        flip = jnp.where(k < 4, k // 2, jnp.where(k == 5, 0, 1))
+        return ((xl + flip) % 2) * NY + (y + turn) % NY
 
     def cols(m):
         return pl.ds(pl.multiple_of(m * COLS, 128), COLS)
@@ -104,7 +110,7 @@
             barrier, inc=1, device_id=device(core, head), device_id_type=pl.DeviceIdType.MESH)
 
     def greet_far(k):
-        m = (k + spot) % NH
+        m = around(k, spot, NH)
         greet(1 - xl, (m // NY) * NP + c * NY + m % NY)
         greet(xl, (m // NY) * NP + (1 - c) * NY + m % NY)
     loop(NH, greet_far)
@@ -115,7 +121,7 @@
     loop(2 * NP - 1, greet_plane)
 
     def greet_depth(k):
-        greet(c, depth(k + 1) * NP + n)
+        greet(c, depth(k) * NP + n)
     loop(NZ - 1, greet_depth)
 
     loads[0].wait()
@@ -145,7 +151,7 @@
         pl.semaphore_wait(barrier, MEET)
 
     def send_query(k):
-        m = (k + spot) % NH
+        m = around(k, spot, NH)
         owner = (m // NY) * NP + c * NY + m % NY
         put(qrows.at[owner], qbuf.at[spot], "Q", 1 - xl, owner)
     loop(NH, send_query)
@@ -166,7 +172,7 @@
     def share(source, landing, phase):
         keep(source(n), landing, phase)
         def step(k):
-            m = plane(k + 1)
+            m = plane(k)
             put(source(m), landing, phase, c, z * NP + m)
         loop(NP - 1, step)
 
@@ -183,16 +189,19 @@
     peak = jnp.max(scores, axis=-1, keepdims=True)
     raw = jnp.exp(scores - peak)
     total = jnp.sum(raw, axis=-1, keepdims=True)
-    latents = jnp.dot(raw.astype(BF16), keys[:, :LAT], preferred_element_type=F32) / total
+    high = raw.astype(BF16)
+    low = (raw - high.astype(F32)).astype(BF16)
+    values = keys[:, :LAT]
+    latents = jnp.dot(high, values, preferred_element_type=F32)
+    latents = (latents + jnp.dot(low, values, preferred_element_type=F32)) / total
     lat_out[...] = latents.reshape(NH, OWN, LAT).astype(BF16)
 
     def send_latent(k):
-        m = (k + spot) % NH
+        m = around(k, spot, NH)
         put(lat_out.at[m], lat_in.at[y // 2, z, y % 2], "LATS",
             xl, (m // NY) * NP + (1 - c) * NY + m % NY)
     loop(NH, send_latent)
 
-    share(lambda m: wg_ref.at[depth_rows(m)], wgu.at[n, half_g, left], "WG")
 
     arrived(wo.at[:, half], "WO")
     put(wo.at[:, half], wo.at[:, half], "WOF", 1 - c, h)
@@ -204,9 +213,11 @@
         head_own[b] = jnp.dot(rows, wuv[...], preferred_element_type=F32).astype(BF16)
         keep(head_own.at[b], head_all.at[b, n], f"HEAD{b}")
         def send_head(k):
-            put(head_own.at[b], head_all.at[b, n], f"HEAD{b}", c, z * NP + plane(k + 1))
+            put(head_own.at[b], head_all.at[b, n], f"HEAD{b}", c, z * NP + plane(k))
         loop(NP - 1, send_head)
 
+    share(lambda m: wg_ref.at[depth_rows(m)], wgu.at[n, half_g, left], "WG")
+    share(lambda m: wu_ref.at[depth_rows(m)], wgu.at[n, half_g, right], "WU")
     arrived(wo.at[:, half], "WOF")
     for b in range(HB):
         arrived(head_all.at[b], f"HEAD{b}")
@@ -215,14 +226,11 @@
         c_out[b] = partial.astype(BF16).reshape(NZ, STRIP, COLS)
         keep(c_out.at[b, z], c_in.at[b, z], f"C{b}")
         def send_c(k):
-            m = depth(k + 1)
+            m = depth(k)
             put(c_out.at[b, m], c_in.at[b, z], f"C{b}", c, m * NP + n)
         loop(NZ - 1, send_c)
 
-    share(lambda m: wu_ref.at[depth_rows(m)], wgu.at[n, half_g, right], "WU")
     share(lambda m: wd_ref.at[half, cols(m)], wd.at[n, half], "WD")
-    arrived(wgu.at[:, half_g, left], "WG")
-    put(wgu.at[:, half_g, left], wgu.at[:, half_g, left], "WGF", 1 - c, h)
 
     def home(core, src, landing, phase, k):
         own = (c == core) & (xl == c) & (y == k)
@@ -246,44 +254,45 @@
         stream = (residual + attended).astype(BF16).astype(F32)
         x_all[b, z] = (stream * gain[...]).astype(BF16)
         def send_x(k):
-            put(x_all.at[b, z], x_all.at[b, z], f"X{b}", c, depth(k + 1) * NP + n)
+            put(x_all.at[b, z], x_all.at[b, z], f"X{b}", c, depth(k) * NP + n)
         loop(NZ - 1, send_x)
 
         squares = jnp.sum(stream * stream, axis=-1, keepdims=True)
-        ssq_own[b] = jnp.broadcast_to(squares, (STRIP, 128))
-        keep(ssq_own.at[b], ssq_in.at[b, n], f"SSQ{b}")
-        def send_ssq(k):
-            put(ssq_own.at[b], ssq_in.at[b, n], f"SSQ{b}", c, z * NP + plane(k + 1))
-        loop(NP - 1, send_ssq)
+        wide = lax.broadcasted_iota(jnp.int32, (STRIP, 128), 1)
+        chosen = selbuf[pair].reshape(STRIP, 128)
+        side_all[b, z] = jnp.where(wide < 8, chosen, squares)
+        def send_side(k):
+            put(side_all.at[b, z], side_all.at[b, z], f"SIDE{b}", c, depth(k) * NP + n)
+        loop(NZ - 1, send_side)
 
         stream_out[pair] = stream.reshape(2, OWN, COLS).astype(BF16)
         home(0, stream_out, stream_in, "STREAM", 2 * b)
         home(0, stream_out, stream_in, "STREAM", 2 * b + 1)
 
-    for b in range(HB):
-        arrived(ssq_in.at[b], f"SSQ{b}")
-        square = ssq_in[b, 0]
-        for i in range(1, NP):
-            square = square + ssq_in[b, i]
-        scale = lax.rsqrt(square * (1.0 / D) + EPS)
-        wide = lax.broadcasted_iota(jnp.int32, (STRIP, 128), 1)
-        chosen = selbuf[2 * b:2 * b + 2].reshape(STRIP, 128)
-        rs_all[b, z] = jnp.where(wide < 8, chosen, scale)
-        def send_rs(k):
-            put(rs_all.at[b, z], rs_all.at[b, z], f"RS{b}", c, depth(k + 1) * NP + n)
-        loop(NZ - 1, send_rs)
-
+    arrived(wgu.at[:, half_g, left], "WG")
+    put(wgu.at[:, half_g, left], wgu.at[:, half_g, left], "WGF", 1 - c, h)
     arrived(wgu.at[:, half_g, right], "WU")
     put(wgu.at[:, half_g, right], wgu.at[:, half_g, right], "WUF", 1 - c, h)
 
     arrived(wgu.at[:, half_g, left], "WGF")
     arrived(wgu.at[:, half_g, right], "WUF")
     others = pl.ds(0, NP - 1)
-    for b in range(HB):
+    lanes = lax.broadcasted_iota(jnp.int32, (PART, 128), 1)
+    gate_of = []
+    for b in range(HB):
+        arrived(side_all.at[b, others], f"SIDE{b}")
+        tiles = side_all[b].reshape(PART, 128)
+        gate_of.append(jnp.sum(jnp.where(lanes == z, tiles, 0.0), axis=-1, keepdims=True))
+        sq_own[b] = jnp.transpose(tiles)[8:16]
+        keep(sq_own.at[b], sq_in.at[b, n], f"SQ{b}")
+        def send_sq(k):
+            put(sq_own.at[b], sq_in.at[b, n], f"SQ{b}", c, z * NP + plane(k))
+        loop(NP - 1, send_sq)
+
         arrived(x_all.at[b, others], f"X{b}")
         x = x_all[b].reshape(PART, COLS)
         def send_h(k):
-            m = plane(k + 1)
+            m = plane(k)
             h_out[b, m] = jnp.dot(x, wgu[m], preferred_element_type=F32).astype(BF16)
             put(h_out.at[b, m], h_in.at[b, n], f"H{b}", c, z * NP + m)
         loop(NP - 1, send_h)
@@ -293,24 +302,24 @@
     arrived(wd.at[:, half], "WD")
     put(wd.at[:, half], wd.at[:, half], "WDF", 1 - c, h)
 
-    lanes = lax.broadcasted_iota(jnp.int32, (PART, 128), 1)
-    gate_of = []
-    for b in range(HB):
-        arrived(rs_all.at[b, others], f"RS{b}")
-        tiles = rs_all[b].reshape(PART, 128)
-        scale = jnp.sum(jnp.where(lanes == 8, tiles, 0.0), axis=-1, keepdims=True)
-        gate_of.append(jnp.sum(jnp.where(lanes == z, tiles, 0.0), axis=-1, keepdims=True))
+    for b in range(HB):
+        arrived(sq_in.at[b], f"SQ{b}")
+        square = sq_in[b, 0]
+        for i in range(1, NP):
+            square = square + sq_in[b, i]
+        scale = lax.rsqrt(square * (1.0 / D) + EPS)
+        scale = jnp.transpose(jnp.broadcast_to(scale[0:1], (128, PART)))
 
         arrived(h_in.at[b], f"H{b}")
         products = h_in[b, 0].astype(F32)
         for i in range(1, NP):
             products = products + h_in[b, i].astype(F32)
-        products = products * scale
-        gated = products[:, :UNITS]
-        hid_own[b] = (gated * jax.nn.sigmoid(gated) * products[:, UNITS:]).astype(BF16)
+        gated = products[:, :UNITS] * scale
+        lifted = products[:, UNITS:] * scale
+        hid_own[b] = (gated * jax.nn.sigmoid(gated) * lifted).astype(BF16)
         keep(hid_own.at[b], hid_all.at[b, n], f"HID{b}")
         def send_hid(k):
-            put(hid_own.at[b], hid_all.at[b, n], f"HID{b}", c, z * NP + plane(k + 1))
+            put(hid_own.at[b], hid_all.at[b, n], f"HID{b}", c, z * NP + plane(k))
         loop(NP - 1, send_hid)
 
     arrived(wd.at[:, half], "WDF")
@@ -321,7 +330,7 @@
         o_out[b] = (expert * gate_of[b]).astype(BF16).reshape(NZ, STRIP, COLS)
         keep(o_out.at[b, z], o_in.at[b, z], f"O{b}")
         def send_o(k):
-            m = depth(k + 1)
+            m = depth(k)
             put(o_out.at[b, m], o_in.at[b, z], f"O{b}", c, m * NP + n)
         loop(NZ - 1, send_o)
 
@@ -362,8 +371,8 @@
     for b in range(HB):
         gone(head_all.at[b, others], f"HEAD{b}")
         gone(c_in.at[b, others], f"C{b}")
-        gone(ssq_in.at[b, others], f"SSQ{b}")
-        gone(rs_all.at[b, others], f"RS{b}")
+        gone(side_all.at[b, others], f"SIDE{b}")
+        gone(sq_in.at[b, others], f"SQ{b}")
         gone(x_all.at[b, others], f"X{b}")
         gone(h_in.at[b, others], f"H{b}")
         gone(hid_all.at[b, others], f"HID{b}")
@@ -409,9 +418,9 @@
         ((HB, NZ, STRIP, COLS), BF16),
         ((NY, OWN, COLS), BF16),
         ((NP, OWN, COLS), BF16),
-        ((HB, STRIP, 128), F32),
-        ((HB, NP, STRIP, 128), F32),
         ((HB, NZ, STRIP, 128), F32),
+        ((HB, 8, PART), F32),
+        ((HB, NP, 8, PART), F32),
         ((HB, NZ, STRIP, COLS), BF16),
         ((HB, NP, PART, 2 * UNITS), BF16),
         ((HB, NP, PART, 2 * UNITS), BF16),

time: 118 us -> 107 us (0.907); the launches traced: 116 us -> 107 us
  Pallas kernels: 114 us -> 105 us
    pallas_call x1, Pallas kernels: 114 us -> 105 us  [per_device(): pl.pallas_call(kernel, out_shape=jax.ShapeDtypeStruct((OWN, D), BF16), in...]
where the time goes in v3:
time: 107 us
  Pallas kernels  105 us (98%)
  local copies, waits for them, and re-layouts  1.55 us (1%)
    pallas_call x1, Pallas kernels, per_device(): pl.pallas_call(kernel, out_shape=jax.ShapeDtypeStruct((OWN, D), BF16), in...  105 us

profile of v3, /device:TPU:25, one launch (start us, length us, event | category | flops | bytes accessed | tf_op | source)
XLA Modules:
  0.0 106.6 jit_solution(5759442660933308765)
XLA Ops:
  0.0 105.0 %layer.1 = bf16[8,7168]{1,0:T(8,128)(2,1)} custom-call(bf16[576,512]{1,0:T(8,128)(2,1)} %bitcast.27, bf16[16,64,576]{2,1,0:T(8,128)(2,1)} %bitcast.26, s32[2,8]{1,0:T(2,128)} %bitcast.33, s32[1,8]{1,0:T(1,128)} %len_ref.1, bf16[512,128]{1,0:T(8,128)(2,1)} %bitcast.28, bf16[128,7168]{1,0:T(8,128)(2,1)} %bitcast.22, bf16[8,7168]{1,0:T(8,128)(2,1)} %bitcast.29, ...), custom_call_target="tpu_custom_call" | custom-call | flops 4000000000 | bytes 16000000 | tf_op jit(solution)/shard_map/layer/pallas_call | solution.py:434
  105.0 1.6 %copy.15 = bf16[1,1,8,7168]{3,2,1,0:T(8,128)(2,1)} copy(bf16[1,1,8,7168]{3,2,1,0:T(8,128)(2,1)} %bitcast.21) | data formatting | bytes 229376

commit v4 on v3

--- a/solution.py
+++ b/solution.py
@@ -30,9 +30,12 @@
 
 
 NAMES = (
-    ["Q", "RES", "SEL", "LATS", "WO", "WOF", "WG", "WGF", "WU", "WUF", "WD", "WDF", "STREAM", "MIX"]
+    ["Q0", "Q1", "RES", "SEL", "LATS", "STREAM", "MIX"]
+    + [name + step for name in ("WO", "WG", "WU", "WD") for step in ("", "F")]
     + [name + str(b) for name in ("HEAD", "C", "SIDE", "SQ", "X", "H", "HID", "O") for b in range(HB)]
 )
+NEAR = 5
+SPANS = ((0, NEAR), (NEAR, NZ))
 PHASE = {name: i for i, name in enumerate(NAMES)}
 
 
@@ -130,6 +133,17 @@
         turned = jnp.transpose(qcols[i:i + wide, :].astype(F32))
         qrows[:, :, i:i + wide] = turned.reshape(64, OWN, wide).astype(BF16)
 
+    with jax.named_scope("w_barrier"):
+        pl.semaphore_wait(barrier, MEET)
+
+    for a, (first, last) in enumerate(SPANS):
+        def send_query(k):
+            p = first + k // NY
+            level = (z + NZ - around(p, 0, NZ)) % NZ
+            owner = level * NP + c * NY + (y + k) % NY
+            put(qrows.at[owner], qbuf.at[p * NY + y], f"Q{a}", 1 - xl, owner)
+        loop((last - first) * NY, send_query)
+
     lane = lax.broadcasted_iota(jnp.int32, (OWN, 128), 1)
     line = lax.broadcasted_iota(jnp.int32, (OWN, 128), 0)
     picked = jnp.zeros((OWN, 128), F32)
@@ -138,6 +152,49 @@
             picked = picked + jnp.where((line == r) & (lane == ids_ref[k, r]), gates_ref[k, r], 0.0)
     sel[...] = picked
 
+    def send_residual(k):
+        m = (1 - c) * NY + (y + k) % NY
+        put(res_ref.at[:, cols(m)], resbuf.at[y], "RES", xl, z * NP + m)
+        put(sel, selbuf.at[y], "SEL", xl, z * NP + m)
+    loop(NY, send_residual)
+
+    left, right = pl.ds(0, UNITS), pl.ds(UNITS, UNITS)
+    arrays = {
+        "WO": (VH, lambda m, i, r: wout_ref.at[r, cols(m)], lambda i, r: wo.at[i, r]),
+        "WG": (COLS, lambda m, i, r: wg_ref.at[i], lambda i, r: wgu.at[i, r, left]),
+        "WU": (COLS, lambda m, i, r: wu_ref.at[i], lambda i, r: wgu.at[i, r, right]),
+        "WD": (UNITS, lambda m, i, r: wd_ref.at[r, cols(m)], lambda i, r: wd.at[i, r]),
+    }
+    every, others = pl.ds(0, NP), pl.ds(0, NP - 1)
+
+    def halves(name):
+        size = arrays[name][0] // 2
+        return pl.ds(pl.multiple_of(c * size, size), size)
+
+    def share(name, first=0, last=NP - 1):
+        depth_of, source, landing = arrays[name]
+        rows = halves(name)
+        size = rows.size
+        place = landing(n, rows)
+        def take(m):
+            deep = pl.ds(pl.multiple_of(m * depth_of + rows.start, size), size)
+            return source(m, deep, rows)
+        if first == 0:
+            keep(take(n), place, name)
+        def step(k):
+            m = plane(k + first)
+            put(take(m), place, name, c, z * NP + m)
+        loop(last - first, step)
+
+    def pass_on(name):
+        mine = arrays[name][2](every, halves(name))
+        arrived(mine, name)
+        put(mine, mine, name + "F", 1 - c, h)
+
+    def ready(name):
+        arrived(arrays[name][2](every, halves(name)), name + "F")
+
+    share("WO")
     row = lax.broadcasted_iota(jnp.int32, (OWN, 1024), 0)
     place = lax.broadcasted_iota(jnp.int32, (OWN, 1024), 1)
     block, offset = place // 64, place % 64
@@ -147,64 +204,36 @@
             (block == tab_ref[1, r]) & (offset + 64 < len_ref[0, r]))
         bias = jnp.where((row == r) & seen, 0.0, bias)
 
-    with jax.named_scope("w_barrier"):
-        pl.semaphore_wait(barrier, MEET)
-
-    def send_query(k):
-        m = around(k, spot, NH)
-        owner = (m // NY) * NP + c * NY + m % NY
-        put(qrows.at[owner], qbuf.at[spot], "Q", 1 - xl, owner)
-    loop(NH, send_query)
-
-    def send_residual(k):
-        m = (1 - c) * NY + (y + k) % NY
-        put(res_ref.at[:, cols(m)], resbuf.at[y], "RES", xl, z * NP + m)
-        put(sel, selbuf.at[y], "SEL", xl, z * NP + m)
-    loop(NY, send_residual)
-
-    half = pl.ds(pl.multiple_of(c * 64, 64), 64)
-    half_g = pl.ds(pl.multiple_of(c * (COLS // 2), COLS // 2), COLS // 2)
-    left, right = pl.ds(0, UNITS), pl.ds(UNITS, UNITS)
-
-    def depth_rows(m):
-        return pl.ds(pl.multiple_of(m * COLS + c * (COLS // 2), COLS // 2), COLS // 2)
-
-    def share(source, landing, phase):
-        keep(source(n), landing, phase)
-        def step(k):
-            m = plane(k)
-            put(source(m), landing, phase, c, z * NP + m)
-        loop(NP - 1, step)
-
-    share(lambda m: wout_ref.at[half, cols(m)], wo.at[n, half], "WO")
 
     loads[1].wait()
-    arrived(qbuf, "Q")
-    queries = qbuf[...].astype(F32).reshape(NH * OWN, KW).astype(BF16)
     keys = pool[...].reshape(1024, KW)
-    scores = lax.dot_general(
-        queries, keys, (((1,), (1,)), ((), ())), preferred_element_type=F32)
-    scores = scores.reshape(NH, OWN, 1024) * SCALE + bias[None]
-    scores = scores.reshape(NH * OWN, 1024)
-    peak = jnp.max(scores, axis=-1, keepdims=True)
-    raw = jnp.exp(scores - peak)
-    total = jnp.sum(raw, axis=-1, keepdims=True)
-    high = raw.astype(BF16)
-    low = (raw - high.astype(F32)).astype(BF16)
     values = keys[:, :LAT]
-    latents = jnp.dot(high, values, preferred_element_type=F32)
-    latents = (latents + jnp.dot(low, values, preferred_element_type=F32)) / total
-    lat_out[...] = latents.reshape(NH, OWN, LAT).astype(BF16)
-
-    def send_latent(k):
-        m = around(k, spot, NH)
-        put(lat_out.at[m], lat_in.at[y // 2, z, y % 2], "LATS",
-            xl, (m // NY) * NP + (1 - c) * NY + m % NY)
-    loop(NH, send_latent)
-
-
-    arrived(wo.at[:, half], "WO")
-    put(wo.at[:, half], wo.at[:, half], "WOF", 1 - c, h)
+    for a, (first, last) in enumerate(SPANS):
+        heads_at_once = (last - first) * NY
+        some = slice(first * NY, last * NY)
+        arrived(qbuf.at[some], f"Q{a}")
+        queries = qbuf[some].astype(F32).reshape(heads_at_once * OWN, KW).astype(BF16)
+        scores = lax.dot_general(
+            queries, keys, (((1,), (1,)), ((), ())), preferred_element_type=F32)
+        scores = scores.reshape(heads_at_once, OWN, 1024) * SCALE + bias[None]
+        scores = scores.reshape(heads_at_once * OWN, 1024)
+        peak = jnp.max(scores, axis=-1, keepdims=True)
+        raw = jnp.exp(scores - peak)
+        total = jnp.sum(raw, axis=-1, keepdims=True)
+        high = raw.astype(BF16)
+        low = (raw - high.astype(F32)).astype(BF16)
+        latents = jnp.dot(high, values, preferred_element_type=F32)
+        latents = (latents + jnp.dot(low, values, preferred_element_type=F32)) / total
+        lat_out[some] = latents.reshape(heads_at_once, OWN, LAT).astype(BF16)
+
+        def send_latent(k):
+            p, m = first + k // NY, (y + k) % NY
+            head = (z + around(p, 0, NZ)) % NZ * NP + (1 - c) * NY + m
+            put(lat_out.at[p * NY + m], lat_in.at[y // 2, z, y % 2], "LATS", xl, head)
+        loop(heads_at_once, send_latent)
+
+    share("WG", 0, 4)
+
 
     loads[2].wait()
     arrived(lat_in, "LATS")
@@ -216,9 +245,10 @@
             put(head_own.at[b], head_all.at[b, n], f"HEAD{b}", c, z * NP + plane(k))
         loop(NP - 1, send_head)
 
-    share(lambda m: wg_ref.at[depth_rows(m)], wgu.at[n, half_g, left], "WG")
-    share(lambda m: wu_ref.at[depth_rows(m)], wgu.at[n, half_g, right], "WU")
-    arrived(wo.at[:, half], "WOF")
+    pass_on("WO")
+    share("WG", 4)
+    share("WU")
+    ready("WO")
     for b in range(HB):
         arrived(head_all.at[b], f"HEAD{b}")
         heads = jnp.concatenate([head_all[b, i] for i in range(NP)], axis=1)
@@ -230,7 +260,7 @@
             put(c_out.at[b, m], c_in.at[b, z], f"C{b}", c, m * NP + n)
         loop(NZ - 1, send_c)
 
-    share(lambda m: wd_ref.at[half, cols(m)], wd.at[n, half], "WD")
+    share("WD")
 
     def home(core, src, landing, phase, k):
         own = (c == core) & (xl == c) & (y == k)
@@ -269,17 +299,15 @@
         home(0, stream_out, stream_in, "STREAM", 2 * b)
         home(0, stream_out, stream_in, "STREAM", 2 * b + 1)
 
-    arrived(wgu.at[:, half_g, left], "WG")
-    put(wgu.at[:, half_g, left], wgu.at[:, half_g, left], "WGF", 1 - c, h)
-    arrived(wgu.at[:, half_g, right], "WU")
-    put(wgu.at[:, half_g, right], wgu.at[:, half_g, right], "WUF", 1 - c, h)
-
-    arrived(wgu.at[:, half_g, left], "WGF")
-    arrived(wgu.at[:, half_g, right], "WUF")
-    others = pl.ds(0, NP - 1)
+    pass_on("WG")
+    pass_on("WU")
+
+    ready("WG")
+    ready("WU")
     lanes = lax.broadcasted_iota(jnp.int32, (PART, 128), 1)
     gate_of = []
-    for b in range(HB):
+
+    def begin(b):
         arrived(side_all.at[b, others], f"SIDE{b}")
         tiles = side_all[b].reshape(PART, 128)
         gate_of.append(jnp.sum(jnp.where(lanes == z, tiles, 0.0), axis=-1, keepdims=True))
@@ -288,21 +316,20 @@
         def send_sq(k):
             put(sq_own.at[b], sq_in.at[b, n], f"SQ{b}", c, z * NP + plane(k))
         loop(NP - 1, send_sq)
-
         arrived(x_all.at[b, others], f"X{b}")
+
+    def lift(b, first, last):
         x = x_all[b].reshape(PART, COLS)
         def send_h(k):
-            m = plane(k)
+            m = plane(k + first)
             h_out[b, m] = jnp.dot(x, wgu[m], preferred_element_type=F32).astype(BF16)
             put(h_out.at[b, m], h_in.at[b, n], f"H{b}", c, z * NP + m)
-        loop(NP - 1, send_h)
-        h_out[b, n] = jnp.dot(x, wgu[n], preferred_element_type=F32).astype(BF16)
-        keep(h_out.at[b, n], h_in.at[b, n], f"H{b}")
-
-    arrived(wd.at[:, half], "WD")
-    put(wd.at[:, half], wd.at[:, half], "WDF", 1 - c, h)
-
-    for b in range(HB):
+        loop(last - first, send_h)
+        if last == NP - 1:
+            h_out[b, n] = jnp.dot(x, wgu[n], preferred_element_type=F32).astype(BF16)
+            keep(h_out.at[b, n], h_in.at[b, n], f"H{b}")
+
+    def join(b):
         arrived(sq_in.at[b], f"SQ{b}")
         square = sq_in[b, 0]
         for i in range(1, NP):
@@ -322,7 +349,15 @@
             put(hid_own.at[b], hid_all.at[b, n], f"HID{b}", c, z * NP + plane(k))
         loop(NP - 1, send_hid)
 
-    arrived(wd.at[:, half], "WDF")
+    begin(0)
+    lift(0, 0, NP - 1)
+    begin(1)
+    lift(1, 0, NP - 1)
+    pass_on("WD")
+    join(0)
+    join(1)
+
+    ready("WD")
     for b in range(HB):
         arrived(hid_all.at[b], f"HID{b}")
         hidden = jnp.concatenate([hid_all[b, i] for i in range(NP)], axis=1)
@@ -356,18 +391,14 @@
     def _():
         finish(mix_in, "MIX")
 
-    gone(qbuf, "Q")
+    for a, (first, last) in enumerate(SPANS):
+        gone(qbuf.at[first * NY:last * NY], f"Q{a}")
     gone(resbuf, "RES")
     gone(selbuf, "SEL")
     gone(lat_in, "LATS")
-    gone(wo.at[others, half], "WO")
-    gone(wo.at[:, half], "WOF")
-    gone(wgu.at[others, half_g, left], "WG")
-    gone(wgu.at[:, half_g, left], "WGF")
-    gone(wgu.at[others, half_g, right], "WU")
-    gone(wgu.at[:, half_g, right], "WUF")
-    gone(wd.at[others, half], "WD")
-    gone(wd.at[:, half], "WDF")
+    for name, (_, _, landing) in arrays.items():
+        gone(landing(others, halves(name)), name)
+        gone(landing(every, halves(name)), name + "F")
     for b in range(HB):
         gone(head_all.at[b, others], f"HEAD{b}")
         gone(c_in.at[b, others], f"C{b}")

time: 107 us -> 103 us (0.963)
  Pallas kernels: 105 us -> 100 us
    pallas_call x1, Pallas kernels: 105 us -> 100 us  [per_device(): pl.pallas_call(kernel, out_shape=jax.ShapeDtypeStruct((OWN, D), BF16), in...]
where the time goes in v4:
time: 103 us; the launch traced here: 102 us
  Pallas kernels  100 us (97%)
  local copies, waits for them, and re-layouts  1.55 us (2%)
    pallas_call x1, Pallas kernels, per_device(): pl.pallas_call(kernel, out_shape=jax.ShapeDtypeStruct((OWN, D), BF16), in...  100 us

profile of v4, /device:TPU:25, one launch (start us, length us, event | category | flops | bytes accessed | tf_op | source)
XLA Modules:
  0.0 101.8 jit_solution(9362440074938070090)
XLA Ops:
  0.0 100.3 %layer.1 = bf16[8,7168]{1,0:T(8,128)(2,1)} custom-call(bf16[576,512]{1,0:T(8,128)(2,1)} %bitcast.27, bf16[16,64,576]{2,1,0:T(8,128)(2,1)} %bitcast.26, s32[2,8]{1,0:T(2,128)} %bitcast.33, s32[1,8]{1,0:T(1,128)} %len_ref.1, bf16[512,128]{1,0:T(8,128)(2,1)} %bitcast.28, bf16[128,7168]{1,0:T(8,128)(2,1)} %bitcast.22, bf16[8,7168]{1,0:T(8,128)(2,1)} %bitcast.29, ...), custom_call_target="tpu_custom_call" | custom-call | flops 4000000000 | bytes 16000000 | tf_op jit(solution)/shard_map/layer/pallas_call | solution.py:465
  100.3 1.6 %copy.15 = bf16[1,1,8,7168]{3,2,1,0:T(8,128)(2,1)} copy(bf16[1,1,8,7168]{3,2,1,0:T(8,128)(2,1)} %bitcast.21) | data formatting | bytes 229376

commit v5 on v4

--- a/solution.py
+++ b/solution.py
@@ -45,8 +45,8 @@
     out_ref,
     qcols, qrows, pool, wuv, gain, qbuf, lat_out, lat_in, sel, resbuf, selbuf,
     wo, wgu, wd, head_own, head_all, c_out, c_in,
-    stream_out, stream_in, side_all, sq_own, sq_in, x_all,
-    h_out, h_in, hid_own, hid_all, o_out, o_in, mix_out, mix_in,
+    stream_out, side_all, sq_own, sq_in, x_all,
+    h_out, h_in, hid_own, hid_all, o_out, o_in, mix_out,
     load, send, recv,
 ):
     c = lax.axis_index("side")
@@ -87,11 +87,11 @@
         return (me + size + far * (2 * (k % 2) - 1)) % size
 
     def depth(k):
-        return around(k + 1, z, NZ)
+        return around(NZ - 1 - k, z, NZ)
 
     def plane(k):
-        turn = jnp.where(k < 4, 1 + 2 * (k % 2), jnp.where(k == 4, 0, 2))
-        flip = jnp.where(k < 4, k // 2, jnp.where(k == 5, 0, 1))
+        turn = jnp.where(k < 2, 2, jnp.where(k < 6, 1 + 2 * (k % 2), 0))
+        flip = jnp.where(k < 2, k, jnp.where(k < 4, 0, 1))
         return ((xl + flip) % 2) * NY + (y + turn) % NY
 
     def cols(m):
@@ -112,11 +112,11 @@
         pl.semaphore_signal(
             barrier, inc=1, device_id=device(core, head), device_id_type=pl.DeviceIdType.MESH)
 
-    def greet_far(k):
-        m = around(k, spot, NH)
-        greet(1 - xl, (m // NY) * NP + c * NY + m % NY)
-        greet(xl, (m // NY) * NP + (1 - c) * NY + m % NY)
-    loop(NH, greet_far)
+    def greet_far(level):
+        for m in range(NY):
+            greet(1 - xl, level * NP + c * NY + m)
+            greet(xl, level * NP + (1 - c) * NY + m)
+    loop(NZ, greet_far)
 
     def greet_plane(k):
         m = (c * NP + n + k + 1) % (2 * NP)
@@ -179,7 +179,7 @@
         def take(m):
             deep = pl.ds(pl.multiple_of(m * depth_of + rows.start, size), size)
             return source(m, deep, rows)
-        if first == 0:
+        if last == NP - 1:
             keep(take(n), place, name)
         def step(k):
             m = plane(k + first)
@@ -232,7 +232,7 @@
             put(lat_out.at[p * NY + m], lat_in.at[y // 2, z, y % 2], "LATS", xl, head)
         loop(heads_at_once, send_latent)
 
-    share("WG", 0, 4)
+    share("WG", 2)
 
 
     loads[2].wait()
@@ -246,7 +246,7 @@
         loop(NP - 1, send_head)
 
     pass_on("WO")
-    share("WG", 4)
+    share("WG", 0, 2)
     share("WU")
     ready("WO")
     for b in range(HB):
@@ -296,8 +296,8 @@
         loop(NZ - 1, send_side)
 
         stream_out[pair] = stream.reshape(2, OWN, COLS).astype(BF16)
-        home(0, stream_out, stream_in, "STREAM", 2 * b)
-        home(0, stream_out, stream_in, "STREAM", 2 * b + 1)
+        home(0, stream_out, out_ref, "STREAM", 2 * b)
+        home(0, stream_out, out_ref, "STREAM", 2 * b + 1)
 
     pass_on("WG")
     pass_on("WU")
@@ -316,9 +316,9 @@
         def send_sq(k):
             put(sq_own.at[b], sq_in.at[b, n], f"SQ{b}", c, z * NP + plane(k))
         loop(NP - 1, send_sq)
+
+    def lift(b, first, last):
         arrived(x_all.at[b, others], f"X{b}")
-
-    def lift(b, first, last):
         x = x_all[b].reshape(PART, COLS)
         def send_h(k):
             m = plane(k + first)
@@ -349,10 +349,10 @@
             put(hid_own.at[b], hid_all.at[b, n], f"HID{b}", c, z * NP + plane(k))
         loop(NP - 1, send_hid)
 
+    lift(0, 0, NP - 1)
     begin(0)
-    lift(0, 0, NP - 1)
+    lift(1, 0, NP - 1)
     begin(1)
-    lift(1, 0, NP - 1)
     pass_on("WD")
     join(0)
     join(1)
@@ -375,21 +375,8 @@
         for i in range(1, NZ):
             mixture = mixture + o_in[b, i].astype(F32)
         mix_out[2 * b:2 * b + 2] = mixture.reshape(2, OWN, COLS).astype(BF16)
-        home(1, mix_out, mix_in, "MIX", 2 * b)
-        home(1, mix_out, mix_in, "MIX", 2 * b + 1)
-
-    def finish(landing, phase):
-        arrived(landing, phase)
-        for i in range(NP):
-            out_ref[:, i * COLS:(i + 1) * COLS] = landing[i]
-
-    @pl.when(c == 0)
-    def _():
-        finish(stream_in, "STREAM")
-
-    @pl.when(c == 1)
-    def _():
-        finish(mix_in, "MIX")
+        home(1, mix_out, out_ref, "MIX", 2 * b)
+        home(1, mix_out, out_ref, "MIX", 2 * b + 1)
 
     for a, (first, last) in enumerate(SPANS):
         gone(qbuf.at[first * NY:last * NY], f"Q{a}")
@@ -420,6 +407,13 @@
 
     gone_home(0, stream_out, "STREAM")
     gone_home(1, mix_out, "MIX")
+    @pl.when(c == 0)
+    def _():
+        arrived(out_ref, "STREAM")
+
+    @pl.when(c == 1)
+    def _():
+        arrived(out_ref, "MIX")
 
 
 def per_device(
@@ -448,7 +442,6 @@
         ((HB, NZ, STRIP, COLS), BF16),
         ((HB, NZ, STRIP, COLS), BF16),
         ((NY, OWN, COLS), BF16),
-        ((NP, OWN, COLS), BF16),
         ((HB, NZ, STRIP, 128), F32),
         ((HB, 8, PART), F32),
         ((HB, NP, 8, PART), F32),
@@ -460,13 +453,12 @@
         ((HB, NZ, STRIP, COLS), BF16),
         ((HB, NZ, STRIP, COLS), BF16),
         ((NY, OWN, COLS), BF16),
-        ((NP, OWN, COLS), BF16),
     ]
     result = pl.pallas_call(
         kernel,
-        out_shape=jax.ShapeDtypeStruct((OWN, D), BF16),
+        out_shape=jax.ShapeDtypeStruct((NP, OWN, COLS), BF16),
         in_specs=[hbm, hbm, smem, smem, hbm, hbm, hbm, hbm, smem, smem, hbm, hbm, hbm],
-        out_specs=pl.BlockSpec(memory_space=pltpu.VMEM),
+        out_specs=hbm,
         scratch_shapes=[pltpu.VMEM(shape, dtype) for shape, dtype in shapes] + [
             pltpu.SemaphoreType.DMA((4,)),
             pltpu.SemaphoreType.DMA((len(NAMES),)),
@@ -482,7 +474,7 @@
         w_uv[0], w_out[0], residual[0], norm_gain.reshape(1, D),
         expert_ids[0].T, expert_gates[0].T, w_gate[0], w_up[0], w_down[0],
     )
-    return result[None, None]
+    return jnp.transpose(result, (1, 0, 2)).reshape(1, 1, OWN, D)
 
 
 def solution(mesh):

time: 103 us -> 99.8 us (0.969)
  Pallas kernels: 100 us -> 97.4 us
    pallas_call x1, Pallas kernels: 100 us -> 97.4 us  [per_device(): pl.pallas_call(kernel, out_shape=jax.ShapeDtypeStruct((NP, OWN, COLS), BF...]
where the time goes in v5:
time: 99.8 us; the launch traced here: 99 us
  Pallas kernels  97.4 us (98%)
  local copies, waits for them, and re-layouts  1.55 us (2%)
    pallas_call x1, Pallas kernels, per_device(): pl.pallas_call(kernel, out_shape=jax.ShapeDtypeStruct((NP, OWN, COLS), BF...  97.4 us

profile of v5, /device:TPU:25, one launch (start us, length us, event | category | flops | bytes accessed | tf_op | source)
XLA Modules:
  0.0 99.0 jit_solution(18394430826071985049)
XLA Ops:
  0.0 97.4 %layer.1 = bf16[8,8,896]{2,1,0:T(8,128)(2,1)} custom-call(bf16[576,512]{1,0:T(8,128)(2,1)} %bitcast.29, bf16[16,64,576]{2,1,0:T(8,128)(2,1)} %bitcast.28, s32[2,8]{1,0:T(2,128)} %bitcast.35, s32[1,8]{1,0:T(1,128)} %len_ref.1, bf16[512,128]{1,0:T(8,128)(2,1)} %bitcast.30, bf16[128,7168]{1,0:T(8,128)(2,1)} %bitcast.24, bf16[8,7168]{1,0:T(8,128)(2,1)} %bitcast.31, ...), custom_call_target="tpu_custom_call" | custom-call | flops 4000000000 | bytes 16000000 | tf_op jit(solution)/shard_map/layer/pallas_call | solution.py:457
  97.4 1.6 %copy.15 = bf16[1,1,8,7168]{3,2,1,0:T(8,128)(2,1)} copy(bf16[1,1,8,7168]{3,2,1,0:T(8,128)(2,1)} %bitcast.23) | data formatting | bytes 229376

commit v6 on v5

--- a/solution.py
+++ b/solution.py
@@ -47,7 +47,7 @@
     wo, wgu, wd, head_own, head_all, c_out, c_in,
     stream_out, side_all, sq_own, sq_in, x_all,
     h_out, h_in, hid_own, hid_all, o_out, o_in, mix_out,
-    load, send, recv,
+    tab, lens, ids, gates, load, send, recv,
 ):
     c = lax.axis_index("side")
     h = lax.axis_index("head")
@@ -102,6 +102,10 @@
         pltpu.make_async_copy(pool_ref, pool, load.at[1]),
         pltpu.make_async_copy(wuv_ref, wuv, load.at[2]),
         pltpu.make_async_copy(gain_ref.at[:, cols(n)], gain, load.at[3]),
+        pltpu.make_async_copy(ids_ref, ids, load.at[4]),
+        pltpu.make_async_copy(gates_ref, gates, load.at[5]),
+        pltpu.make_async_copy(tab_ref, tab, load.at[6]),
+        pltpu.make_async_copy(len_ref, lens, load.at[7]),
     ]
     for copy in loads:
         copy.start()
@@ -147,9 +151,11 @@
     lane = lax.broadcasted_iota(jnp.int32, (OWN, 128), 1)
     line = lax.broadcasted_iota(jnp.int32, (OWN, 128), 0)
     picked = jnp.zeros((OWN, 128), F32)
+    loads[4].wait()
+    loads[5].wait()
     for r in range(OWN):
-        for k in range(ids_ref.shape[0]):
-            picked = picked + jnp.where((line == r) & (lane == ids_ref[k, r]), gates_ref[k, r], 0.0)
+        for k in range(ids.shape[0]):
+            picked = picked + jnp.where((line == r) & (lane == ids[k, r]), gates[k, r], 0.0)
     sel[...] = picked
 
     def send_residual(k):
@@ -199,9 +205,11 @@
     place = lax.broadcasted_iota(jnp.int32, (OWN, 1024), 1)
     block, offset = place // 64, place % 64
     bias = jnp.full((OWN, 1024), -1e30, F32)
+    loads[6].wait()
+    loads[7].wait()
     for r in range(OWN):
-        seen = ((block == tab_ref[0, r]) & (offset < len_ref[0, r])) | (
-            (block == tab_ref[1, r]) & (offset + 64 < len_ref[0, r]))
+        seen = ((block == tab[0, r]) & (offset < lens[0, r])) | (
+            (block == tab[1, r]) & (offset + 64 < lens[0, r]))
         bias = jnp.where((row == r) & seen, 0.0, bias)
 
 
@@ -296,8 +304,6 @@
         loop(NZ - 1, send_side)
 
         stream_out[pair] = stream.reshape(2, OWN, COLS).astype(BF16)
-        home(0, stream_out, out_ref, "STREAM", 2 * b)
-        home(0, stream_out, out_ref, "STREAM", 2 * b + 1)
 
     pass_on("WG")
     pass_on("WU")
@@ -368,6 +374,9 @@
             m = depth(k)
             put(o_out.at[b, m], o_in.at[b, z], f"O{b}", c, m * NP + n)
         loop(NZ - 1, send_o)
+
+    for k in range(NY):
+        home(0, stream_out, out_ref, "STREAM", k)
 
     for b in range(HB):
         arrived(o_in.at[b], f"O{b}")
@@ -421,7 +430,6 @@
     expert_ids, expert_gates, w_gate, w_up, w_down,
 ):
     hbm = pl.BlockSpec(memory_space=pl.ANY)
-    smem = pl.BlockSpec(memory_space=pltpu.SMEM)
     shapes = [
         ((KW, 512), BF16),
         ((64, OWN, KW), BF16),
@@ -457,10 +465,14 @@
     result = pl.pallas_call(
         kernel,
         out_shape=jax.ShapeDtypeStruct((NP, OWN, COLS), BF16),
-        in_specs=[hbm, hbm, smem, smem, hbm, hbm, hbm, hbm, smem, smem, hbm, hbm, hbm],
+        in_specs=[hbm] * 13,
         out_specs=hbm,
         scratch_shapes=[pltpu.VMEM(shape, dtype) for shape, dtype in shapes] + [
-            pltpu.SemaphoreType.DMA((4,)),
+            pltpu.SMEM((2, OWN), jnp.int32),
+            pltpu.SMEM((1, OWN), jnp.int32),
+            pltpu.SMEM((4, OWN), jnp.int32),
+            pltpu.SMEM((4, OWN), F32),
+            pltpu.SemaphoreType.DMA((8,)),
             pltpu.SemaphoreType.DMA((len(NAMES),)),
             pltpu.SemaphoreType.DMA((len(NAMES),)),
         ],

time: 99.8 us -> 97.6 us (0.978)
  Pallas kernels: 97.4 us -> 96 us
    pallas_call x1, Pallas kernels: 97.4 us -> 96 us  [per_device(): pl.pallas_call(kernel, out_shape=jax.ShapeDtypeStruct((NP, OWN, COLS), BF...]
where the time goes in v6:
time: 97.6 us; the launch traced here: 97.5 us
  Pallas kernels  96 us (98%)
  local copies, waits for them, and re-layouts  1.55 us (2%)
    pallas_call x1, Pallas kernels, per_device(): pl.pallas_call(kernel, out_shape=jax.ShapeDtypeStruct((NP, OWN, COLS), BF...  96 us

profile of v6, /device:TPU:25, one launch (start us, length us, event | category | flops | bytes accessed | tf_op | source)
XLA Modules:
  0.0 97.5 jit_solution(1294456101583005619)
XLA Ops:
  0.0 96.0 %layer.1 = bf16[8,8,896]{2,1,0:T(8,128)(2,1)} custom-call(bf16[576,512]{1,0:T(8,128)(2,1)} %bitcast.29, bf16[16,64,576]{2,1,0:T(8,128)(2,1)} %bitcast.28, s32[2,8]{1,0:T(2,128)} %bitcast.35, s32[1,8]{1,0:T(1,128)} %len_ref.1, bf16[512,128]{1,0:T(8,128)(2,1)} %bitcast.30, bf16[128,7168]{1,0:T(8,128)(2,1)} %bitcast.24, bf16[8,7168]{1,0:T(8,128)(2,1)} %bitcast.31, ...), custom_call_target="tpu_custom_call" | custom-call | flops 4000000000 | bytes 16000000 | tf_op jit(solution)/shard_map/layer/pallas_call | solution.py:465
  96.0 1.6 %copy.15 = bf16[1,1,8,7168]{3,2,1,0:T(8,128)(2,1)} copy(bf16[1,1,8,7168]{3,2,1,0:T(8,128)(2,1)} %bitcast.23) | data formatting | bytes 229376

commit v7 on v6

--- a/solution.py
+++ b/solution.py
@@ -125,11 +125,11 @@
     def greet_plane(k):
         m = (c * NP + n + k + 1) % (2 * NP)
         greet(m // NP, z * NP + m % NP)
-    loop(2 * NP - 1, greet_plane)
-
-    def greet_depth(k):
-        greet(c, depth(k) * NP + n)
-    loop(NZ - 1, greet_depth)
+    for k in range(2 * NP - 1):
+        greet_plane(k)
+
+    for k in range(1, NZ):
+        greet(c, (z + k) % NZ * NP + n)
 
     loads[0].wait()
     for i in range(0, KW, 128):

time: 97.6 us -> 97.6 us (level)
  no operation moved by 1% of the time
where the time goes in v7:
time: 97.6 us; the launch traced here: 97.4 us
  Pallas kernels  95.8 us (98%)
  local copies, waits for them, and re-layouts  1.55 us (2%)
    pallas_call x1, Pallas kernels, per_device(): pl.pallas_call(kernel, out_shape=jax.ShapeDtypeStruct((NP, OWN, COLS), BF...  95.8 us

profile of v7, /device:TPU:25, one launch (start us, length us, event | category | flops | bytes accessed | tf_op | source)
XLA Modules:
  0.0 97.4 jit_solution(1446566774274098980)
XLA Ops:
  0.0 95.8 %layer.1 = bf16[8,8,896]{2,1,0:T(8,128)(2,1)} custom-call(bf16[576,512]{1,0:T(8,128)(2,1)} %bitcast.29, bf16[16,64,576]{2,1,0:T(8,128)(2,1)} %bitcast.28, s32[2,8]{1,0:T(2,128)} %bitcast.35, s32[1,8]{1,0:T(1,128)} %len_ref.1, bf16[512,128]{1,0:T(8,128)(2,1)} %bitcast.30, bf16[128,7168]{1,0:T(8,128)(2,1)} %bitcast.24, bf16[8,7168]{1,0:T(8,128)(2,1)} %bitcast.31, ...), custom_call_target="tpu_custom_call" | custom-call | flops 4000000000 | bytes 16000000 | tf_op jit(solution)/shard_map/layer/pallas_call | solution.py:465
  95.8 1.6 %copy.15 = bf16[1,1,8,7168]{3,2,1,0:T(8,128)(2,1)} copy(bf16[1,1,8,7168]{3,2,1,0:T(8,128)(2,1)} %bitcast.23) | data formatting | bytes 229376
